TPU v7x, 128 devices: a whole 4x4x4 slice. The times are simulated.
128 devices in a mesh: req: 8 (over z, core), cache: 16 (over y, x).
Axes of the slice: x: 4, y: 4, z: 4, core: 2. Of those that a mesh axis runs over, the one named last changes fastest.
Arguments:
- event_feats: bfloat16 [128, 512, 1024], P(('req', 'cache')), may hold values from -6 to 6
- hist_len: int32 [128, 16], P(('req', 'cache')), may hold values from 1 to 64, 512 in all within a row
- user_owner: int32 [128, 16], P(('req', 'cache')), may hold values from 0 to 15, each once within a row
- cand_ids: int32 [128, 1024], P(('req', 'cache')), may hold values from 0 to 1023
- cand_count: int32 [128, 8], P(('req', 'cache')), may hold values from 1 to 128, 512 in all within a row
- req_owner: int32 [128, 8], P(('req', 'cache')), may hold values from 0 to 7, each once within a row
- req_slot: int32 [128, 8], P(('req', 'cache')), may hold values from 0 to 15
- table: bfloat16 [1024, 1024], replicated, may hold values from -6 to 6
- w_qu: bfloat16 [1024, 2048], replicated, may hold values from -0.1875 to 0.1875
- w_kv: bfloat16 [1024, 2048], replicated, may hold values from -0.1875 to 0.1875
- w_out: bfloat16 [1024, 1024], replicated, may hold values from -0.1875 to 0.1875
Outputs:
- cache_kv: bfloat16 [128, 16, 64, 2048], P(('req', 'cache'))
- cand_out: bfloat16 [128, 1024, 1024], P(('req', 'cache'))
Inputs may be any that keep to these rules, and one draw needn't show every extreme that they name: `hist_len`: each device's users together hold exactly 512 events. `user_owner`: each row names every index along cache once. `req_owner`: each row names every index along req once.
All inputs are finite; a program needn't handle non-finite values.
Results may differ from a plain program's by a relative error of at most 0.0063.
Values may be sent and summed in bfloat16 or wider, within the bound.
A program may use at most 128 MiB of HBM per device.

v0:
```python
import jax
import jax.numpy as jnp
from jax import lax
from jax.sharding import PartitionSpec as P

D = 1024
HEADS = 8
HEAD_DIM = 128
HIST = 64
CB = 128


def layer_norm(values):
    mean = jnp.mean(values, axis=-1, keepdims=True)
    centred = values - mean
    spread = jnp.mean(centred * centred, axis=-1, keepdims=True)
    return centred * lax.rsqrt(spread + 1e-06)


def norm_rows(values):
    return layer_norm(values.astype(jnp.float32)).astype(jnp.bfloat16)


def embed_rows(row_ids, table):
    embedded = jnp.take(table, row_ids, axis=0)
    return (embedded, norm_rows(embedded))


def silu_proj(normed, weight):
    return jax.nn.silu(jnp.dot(normed, weight, preferred_element_type=jnp.float32)).astype(
        jnp.bfloat16
    )


def history_attend(queries, blocks):
    block_count = queries.shape[0]
    block_rows = queries.shape[1]
    query_heads = queries.reshape(block_count, block_rows, HEADS, HEAD_DIM)
    key_heads = blocks[:, :, :D].reshape(block_count, HIST, HEADS, HEAD_DIM)
    value_heads = blocks[:, :, D:].reshape(block_count, HIST, HEADS, HEAD_DIM)
    scores = jnp.einsum(
        "rihd,rthd->rhit", query_heads, key_heads, preferred_element_type=jnp.float32
    ) * HEAD_DIM ** (-0.5)
    weights = jax.nn.silu(scores).astype(jnp.bfloat16)
    mixed = jnp.einsum("rhit,rthd->rihd", weights, value_heads, preferred_element_type=jnp.float32)
    return mixed.reshape(block_count, block_rows, D).astype(jnp.bfloat16)


def finish(embedded, query_gate, keys_vals, hist_att, counts, w_out):
    query_heads = query_gate[:, :D].astype(jnp.float32).reshape(-1, HEADS, HEAD_DIM)
    key_heads = keys_vals[:, :D].astype(jnp.float32).reshape(-1, HEADS, HEAD_DIM)
    value_heads = keys_vals[:, D:].astype(jnp.float32).reshape(-1, HEADS, HEAD_DIM)
    self_weight = jax.nn.silu(jnp.sum(query_heads * key_heads, axis=-1) * HEAD_DIM ** (-0.5))
    self_term = (self_weight[..., None] * value_heads).reshape(-1, D)
    attended = hist_att.astype(jnp.float32) + self_term
    gated = (layer_norm(attended) * query_gate[:, D:].astype(jnp.float32)).astype(jnp.bfloat16)
    result = jnp.dot(gated, w_out, preferred_element_type=jnp.float32) + embedded.astype(
        jnp.float32
    )
    slot_ids = jnp.arange(result.shape[0], dtype=jnp.int32)
    live_rows = slot_ids % CB < counts[slot_ids // CB]
    return jnp.where(live_rows[:, None], result, 0.0).astype(jnp.bfloat16)


def body(
    event_feats,
    hist_len,
    user_owner,
    cand_ids,
    cand_count,
    req_owner,
    req_slot,
    table,
    w_qu,
    w_kv,
    w_out,
):
    n_cache = lax.axis_size("cache")
    feats = event_feats[0]
    pre_rows = feats.shape[0]
    lengths = hist_len[0]
    owners = user_owner[0]
    starts = jnp.cumsum(lengths) - lengths
    picked = jnp.argmax(owners[None, :] == jnp.arange(n_cache, dtype=jnp.int32)[:, None], axis=1)
    send_start = starts[picked]
    send_len = lengths[picked]
    positions = jnp.arange(HIST, dtype=jnp.int32)
    live_mask = positions[None, :] < send_len[:, None]
    row_index = jnp.clip(send_start[:, None] + positions[None, :], 0, pre_rows - 1)
    zero_value = jnp.zeros((), jnp.bfloat16)
    packed_kv = silu_proj(norm_rows(feats), w_kv)
    outgoing = jnp.where(live_mask[..., None], jnp.take(packed_kv, row_index, axis=0), zero_value)
    cached = lax.all_to_all(outgoing, "cache", split_axis=0, concat_axis=0, tiled=True)
    requests = req_owner.shape[1]
    owner_of = req_owner[0]
    slot_of = req_slot[0]
    cand_emb, cand_norm = embed_rows(cand_ids[0], table)
    query_gate = silu_proj(cand_norm, w_qu)
    keys_vals = silu_proj(cand_norm, w_kv)
    queries = query_gate[:, :D].reshape(requests, CB, D)
    ordering = jnp.argmax(
        owner_of[None, :] == jnp.arange(requests, dtype=jnp.int32)[:, None], axis=1
    )
    send_queries = queries[ordering]
    send_slots = slot_of[ordering]
    slot_rows = jnp.broadcast_to(send_slots[:, None], (requests, CB))
    arrived = lax.all_to_all(send_queries, "req", split_axis=0, concat_axis=0, tiled=True)
    slot_piece = lax.all_to_all(slot_rows, "req", split_axis=0, concat_axis=0, tiled=True)
    blocks = cached[slot_piece[:, 0]]
    answer = history_attend(arrived, blocks)
    returned = lax.all_to_all(answer, "req", split_axis=0, concat_axis=0, tiled=True)
    hist_att = returned[owner_of]
    cand_out = finish(
        cand_emb, query_gate, keys_vals, hist_att.reshape(requests * CB, D), cand_count[0], w_out
    )
    return (cached[None], cand_out[None])


def solution(mesh):
    in_specs = (
        P(("req", "cache"), None, None),
        P(("req", "cache"), None),
        P(("req", "cache"), None),
        P(("req", "cache"), None),
        P(("req", "cache"), None),
        P(("req", "cache"), None),
        P(("req", "cache"), None),
        P(),
        P(),
        P(),
        P(),
    )
    out_specs = (P(("req", "cache"), None, None, None), P(("req", "cache"), None, None))
    return jax.shard_map(body, mesh=mesh, in_specs=in_specs, out_specs=out_specs, check_vma=False)
```

profile of v0, /device:TPU:1, one launch (start us, length us, event | category | flops | bytes accessed | tf_op | source)
XLA Modules:
  0.0 211.5 jit_solution(16760191870360175252)
XLA Ops:
  0.6 0.0 copy-start
  0.6 1.4 iota_reduce_fusion.1
  2.1 1.3 gather_fusion.3
  3.4 0.7 broadcast_in_dim.90
  4.1 6.8 %all-to-all-start.1 = ((s32[8,1,128]{2,1,0:T(1,128)}), s32[8,1,128]{2,1,0:T(1,128)S(1)}, u32[]{:S(2)}, u32[]{:S(2)}) async-start(s32[8,1,128]{2,1,0:T(1,128)} %broadcast_in_dim.90), calls=%async_computation.1 | async-start | bytes 8192 | tf_op jit(solution)/shard_map/all_to_all | solution.py:108
  10.9 1.3 iota_reduce_fusion
  12.2 1.4 convert_reduce_fusion.1
  13.6 1.6 fusion.10
  15.3 0.7 compare_select_fusion
  16.0 1.6 fusion.52
  17.6 0.7 copy.47
  18.4 0.1 reduce.37
  18.5 0.7 bitcast_subtract_fusion
  19.2 0.7 gather_fusion.1
  19.8 0.1 compare_select_fusion.2
  19.9 0.1 reshape.327
  20.0 0.0 copy-start.11
  20.0 5.3 %gather_fusion.5 = bf16[1024,1024]{1,0:T(8,128)(2,1)} fusion(bf16[1024,1024]{1,0:T(8,128)(2,1)S(1)} %copy-done, s32[1024]{0:T(1024)S(1)} %broadcast_clamp_fusion), kind=kCustom, calls=%fused_computation.5 | custom fusion | bytes 4198400 | tf_op jit(solution)/shard_map/jit(_take)/gather | solution.py:25
  25.4 4.4 %compare_select_fusion.4 = s32[1024,1]{0,1:T(1,128)S(1)} fusion(s32[]{:T(128)} %bitcast.7, s32[]{:T(128)} %bitcast.8, s32[]{:T(128)} %bitcast.9, s32[]{:T(128)} %bitcast.10, s32[]{:T(128)} %bitcast.11, s32[]{:T(128)} %bitcast.13, s32[]{:T(128)} %bitcast.12), kind=kLoop, calls=%fused_computation.58 | loop fusion | flops 23552 | bytes 4124 | tf_op jit(solution)/shard_map/gather | solution.py:61
  29.8 0.7 fusion.34
  30.5 2.2 %convert_reduce_fusion = f32[1024]{0:T(1024)S(1)} fusion(bf16[1024,1024]{1,0:T(8,128)(2,1)} %gather_fusion.5, pred[1024]{0:T(1024)(128)(4,1)S(1)} %get-tuple-element.21), kind=kLoop, calls=%fused_computation.12 | loop fusion | flops 3144704 | bytes 2102272 | tf_op jit(solution)/shard_map/reduce_sum | solution.py:14
  32.7 2.4 %fusion.2 = f32[1024]{0:T(1024)S(1)} fusion(f32[1024]{0:T(1024)S(1)} %broadcast_multiply_fusion.1, bf16[1024,1024]{1,0:T(8,128)(2,1)} %gather_fusion.5, pred[1024]{0:T(1024)(128)(4,1)S(1)} %get-tuple-element.21), kind=kLoop, calls=%fused_computation.15 | loop fusion | flops 5241856 | bytes 2106368 | tf_op jit(solution)/shard_map/reduce_sum | solution.py:16
  35.2 0.0 copy-start.2
  35.2 9.7 %multiply_convert_fusion.1 = bf16[1024,2048]{1,0:T(8,128)(2,1)} fusion(bf16[1024,2048]{1,0:T(8,128)(2,1)} %param.19, f32[1024]{0:T(1024)S(1)} %add_rsqrt_fusion.1, f32[1024]{0:T(1024)S(1)} %broadcast_multiply_fusion.1, bf16[1024,1024]{1,0:T(8,128)(2,1)S(1)} %copy-done.3, pred[1024]{0:T(1024)(128)(4,1)S(1)} %get-tuple-element.21), kind=kOutput, calls=%fused_computation.9 | convolution fusion | flops 4310695936 | bytes 10494976 | tf_op jit(solution)/shard_map/dot_general | solution.py:30
  44.9 0.7 gather_fusion
  45.5 0.9 slice-done
  46.4 2.0 gather_fusion.6
  48.4 4.8 %all-to-all-start.2 = ((bf16[8,128,1024]{2,1,0:T(8,128)(2,1)}), bf16[8,128,1024]{2,1,0:T(8,128)(2,1)}, u32[]{:S(2)}, u32[]{:S(2)}) async-start(bf16[8,128,1024]{2,1,0:T(8,128)(2,1)} %gather_fusion.6), calls=%async_computation.2 | async-start | bytes 4194304 | tf_op jit(solution)/shard_map/all_to_all | solution.py:107
  53.3 5.1 %multiply_convert_fusion.3 = bf16[512,2048]{1,0:T(8,128)(2,1)S(1)} fusion(bf16[1024,2048]{1,0:T(8,128)(2,1)} %param.20, bf16[1,512,1024]{2,1,0:T(8,128)(2,1)S(1)} %copy-done.8, f32[512]{0:T(512)S(1)} %add_rsqrt_fusion.2, f32[512]{0:T(512)S(1)} %broadcast_multiply_fusion.2), kind=kOutput, calls=%fused_computation.25 | convolution fusion | flops 2154823680 | bytes 7344128 | tf_op jit(solution)/shard_map/dot_general | solution.py:30
  58.3 6.0 %gather_fusion.2 = bf16[1024,2048]{1,0:T(8,128)(2,1)} fusion(bf16[512,2048]{1,0:T(8,128)(2,1)S(1)} %multiply_convert_fusion.3, s32[1024]{0:T(1024)S(1)} %broadcast_clamp_fusion.1), kind=kCustom, calls=%fused_computation.2 | custom fusion | bytes 8392704 | tf_op jit(solution)/shard_map/jit(_take)/gather | solution.py:92
  64.3 0.1 iota_compare_fusion.1
  64.4 3.9 %select_select_fusion = bf16[16,64,2048]{2,1,0:T(8,128)(2,1)} fusion(bf16[16,64,2048]{2,1,0:T(8,128)(2,1)} %bitcast.84, pred[16,64]{1,0:T(8,128)(4,1)S(1)} %get-tuple-element.19, pred[16,64]{1,0:T(8,128)(4,1)S(1)} %get-tuple-element.18), kind=kLoop, calls=%fused_computation.24 | loop fusion | flops 4194304 | bytes 8390656 | tf_op jit(solution)/shard_map/jit(_where)/select_n | solution.py:92
  68.3 11.4 %all-to-all-done.2 = bf16[8,128,1024]{2,1,0:T(8,128)(2,1)} async-done(((bf16[8,128,1024]{2,1,0:T(8,128)(2,1)}), bf16[8,128,1024]{2,1,0:T(8,128)(2,1)}, u32[]{:S(2)}, u32[]{:S(2)}) %all-to-all-start.2) | async-done | bytes 2097184 | tf_op jit(solution)/shard_map/all_to_all | solution.py:107
  79.7 6.8 %all-to-all-start = ((bf16[16,64,2048]{2,1,0:T(8,128)(2,1)}), bf16[16,64,2048]{2,1,0:T(8,128)(2,1)}, u32[]{:S(2)}, u32[]{:S(2)}) async-start(bf16[16,64,2048]{2,1,0:T(8,128)(2,1)} %select_select_fusion), calls=%async_computation | async-start | bytes 8388608 | tf_op jit(solution)/shard_map/all_to_all | solution.py:93
  86.5 0.1 copy.48
  86.6 3.9 %copy.49 = bf16[8,128,1024]{1,2,0:T(8,128)(2,1)} copy(bf16[8,128,1024]{2,1,0:T(8,128)(2,1)} %all-to-all-done.2) | data formatting | bytes 4194304 | tf_op jit(solution)/shard_map/all_to_all | solution.py:107
  90.6 57.7 %all-to-all-done = bf16[16,64,2048]{2,1,0:T(8,128)(2,1)} async-done(((bf16[16,64,2048]{2,1,0:T(8,128)(2,1)}), bf16[16,64,2048]{2,1,0:T(8,128)(2,1)}, u32[]{:S(2)}, u32[]{:S(2)}) %all-to-all-start) | async-done | bytes 4194336 | tf_op jit(solution)/shard_map/all_to_all | solution.py:93
  148.3 2.9 %gather_fusion.4 = bf16[8,64,2048]{2,1,0:T(8,128)(2,1)S(1)} fusion(bf16[16,64,2048]{2,1,0:T(8,128)(2,1)} %all-to-all-done, s32[1024]{0:T(1024)S(1)} %pad_clamp_fusion.1), kind=kCustom, calls=%fused_computation.4 | custom fusion | bytes 4194336 | tf_op jit(solution)/shard_map/gather | solution.py:109
  151.2 1.2 slice_bitcast_fusion.1
  152.4 4.6 %convolution_convert_fusion = bf16[8,8,128,128]{3,2,1,0:T(8,128)(2,1)} fusion(bf16[8,128,8,128]{1,3,2,0:T(8,128)(2,1)} %bitcast.88, bf16[8,8,8,8,128]{4,3,2,1,0:T(8,128)(2,1)} %get-tuple-element.9, bf16[8,8,8,8,128]{4,3,2,1,0:T(8,128)(2,1)S(1)} %get-tuple-element.8), kind=kOutput, calls=%fused_computation.40 | convolution fusion | flops 272629760 | bytes 6291456 | tf_op jit(solution)/shard_map/rhit,rthd->rihd/dot_general | solution.py:45
  157.0 4.1 %copy.53 = bf16[8,128,1024]{2,1,0:T(8,128)(2,1)} copy(bf16[8,128,1024]{1,2,0:T(8,128)(2,1)} %bitcast.89) | data formatting | bytes 4194304 | tf_op jit(solution)/shard_map/convert_element_type | solution.py:46
  161.1 6.3 %all-to-all-start.3 = ((bf16[8,128,1024]{2,1,0:T(8,128)(2,1)}), bf16[8,128,1024]{2,1,0:T(8,128)(2,1)}, u32[]{:S(2)}, u32[]{:S(2)}) async-start(bf16[8,128,1024]{2,1,0:T(8,128)(2,1)} %copy.53), calls=%async_computation.3 | async-start | bytes 4194304 | tf_op jit(solution)/shard_map/all_to_all | solution.py:111
  167.4 8.5 %multiply_convert_fusion = bf16[1024,2048]{1,0:T(8,128)(2,1)S(1)} fusion(bf16[1024,2048]{1,0:T(8,128)(2,1)} %param.20, f32[1024]{0:T(1024)S(1)} %add_rsqrt_fusion.1, f32[1024]{0:T(1024)S(1)} %broadcast_multiply_fusion.1, bf16[1024,1024]{1,0:T(8,128)(2,1)S(1)} %copy-done.4, pred[1024]{0:T(1024)(128)(4,1)S(1)} %get-tuple-element.21), kind=kOutput, calls=%fused_computation.8 | convolution fusion | flops 4310695936 | bytes 10494976 | tf_op jit(solution)/shard_map/dot_general | solution.py:30
  175.9 0.0 copy-start.9
  175.9 1.0 multiply_bitcast_fusion
  176.9 1.0 copy-done.9
  177.9 3.0 %copy.59 = f32[128,8,8,128]{3,2,1,0:T(8,128)} copy(f32[128,8,8,128]{3,1,2,0:T(8,128)S(1)} %multiply_bitcast_fusion) | data formatting | bytes 8388608
  180.9 3.4 %reduce_sum.67 = f32[1024,8]{1,0:T(8,128)S(1)} reduce(f32[1024,8,128]{2,1,0:T(8,128)} %bitcast.86, f32[]{:T(128)} %constant.97.clone.1), dimensions={2}, to_apply=%region_7.8 | reduce | flops 1040384 | bytes 4227076 | tf_op jit(solution)/shard_map/reduce_sum | solution.py:53
  184.3 0.2 copy.54
  184.5 0.2 copy.55
  184.7 9.1 %all-to-all-done.3 = bf16[8,128,1024]{2,1,0:T(8,128)(2,1)} async-done(((bf16[8,128,1024]{2,1,0:T(8,128)(2,1)}), bf16[8,128,1024]{2,1,0:T(8,128)(2,1)}, u32[]{:S(2)}, u32[]{:S(2)}) %all-to-all-start.3) | async-done | bytes 2097184 | tf_op jit(solution)/shard_map/all_to_all | solution.py:111
  193.8 2.3 %gather_fusion.7 = bf16[8,128,1024]{2,1,0:T(8,128)(2,1)S(1)} fusion(bf16[8,128,1024]{2,1,0:T(8,128)(2,1)} %all-to-all-done.3, s32[1024]{0:T(1024)S(1)} %pad_clamp_fusion), kind=kCustom, calls=%fused_computation.7 | custom fusion | bytes 4194336 | tf_op jit(solution)/shard_map/gather | solution.py:112
  196.1 0.0 copy-start.10
  196.1 1.1 mul.109
  197.2 1.0 copy-done.10
  198.3 1.2 fusion.50
  199.5 0.0 copy-start.5
  199.5 0.0 copy-start.12
  199.5 0.6 multiply_reduce_fusion
  200.1 0.4 copy-done.7
  200.5 0.9 copy-done.5
  201.4 0.6 copy-done.12
  202.0 4.7 %fusion.13 = bf16[1,1024,1024]{2,1,0:T(8,128)(2,1)} fusion(pred[1024]{0:T(1024)(128)(4,1)S(1)} %get-tuple-element.20, bf16[1024,1024]{1,0:T(8,128)(2,1)S(1)} %copy-done.12, f32[1024,1024]{1,0:T(8,128)S(1)} %get-tuple-element.7, bf16[1024,2048]{1,0:T(8,128)(2,1)S(1)} %copy-done.7, f32[1024]{0:T(1024)S(1)} %add_rsqrt_fusion, ...), kind=kOutput, calls=%fused_computation.34 | convolution fusion | flops 2157969408 | bytes 12593152 | tf_op jit(solution)/shard_map/dot_general | solution.py:57
  206.7 4.8 %copy.73 = bf16[1,16,64,2048]{3,2,1,0:T(8,128)(2,1)} copy(bf16[1,16,64,2048]{3,2,1,0:T(8,128)(2,1)} %bitcast.5) | data formatting | bytes 8388608
  (37 shorter events, 0.2 us)
Async XLA Ops:
  0.6 19.4 %copy-start = (bf16[1024,1024]{1,0:T(8,128)(2,1)S(1)}, bf16[1024,1024]{1,0:T(8,128)(2,1)}, u32[]{:S(2)}) copy-start(bf16[1024,1024]{1,0:T(8,128)(2,1)} %param.18) | copy-start | bytes 6291460
  4.1 44.4 %all-to-all-start.1 = ((s32[8,1,128]{2,1,0:T(1,128)}), s32[8,1,128]{2,1,0:T(1,128)S(1)}, u32[]{:S(2)}, u32[]{:S(2)}) async-start(s32[8,1,128]{2,1,0:T(1,128)} %broadcast_in_dim.90), calls=%async_computation.1 | async-start | bytes 8192 | tf_op jit(solution)/shard_map/all_to_all | solution.py:108
  20.0 9.8 %copy-start.11 = (s32[1,1024]{1,0:T(1,128)S(1)}, s32[1,1024]{1,0:T(1,128)}, u32[]{:S(2)}) copy-start(s32[1,1024]{1,0:T(1,128)} %param.14) | copy-start | bytes 12292
  25.3 9.8 %copy-start.3 = (bf16[1024,1024]{1,0:T(8,128)(2,1)S(1)}, bf16[1024,1024]{1,0:T(8,128)(2,1)}, u32[]{:S(2)}) copy-start(bf16[1024,1024]{1,0:T(8,128)(2,1)} %gather_fusion.5) | copy-start | bytes 6291460
  35.2 9.7 %copy-start.2 = (s32[1,16]{1,0:T(1,128)S(1)}, s32[1,16]{1,0:T(1,128)}, u32[]{:S(2)}) copy-start(s32[1,16]{1,0:T(1,128)} %param.12) | copy-start | bytes 196
  44.8 1.6 slice-start
  46.4 6.8 %copy-start.8 = (bf16[1,512,1024]{2,1,0:T(8,128)(2,1)S(1)}, bf16[1,512,1024]{2,1,0:T(8,128)(2,1)}, u32[]{:S(2)}) copy-start(bf16[1,512,1024]{2,1,0:T(8,128)(2,1)} %param.11) | copy-start | bytes 3145732
  48.4 31.2 %all-to-all-start.2 = ((bf16[8,128,1024]{2,1,0:T(8,128)(2,1)}), bf16[8,128,1024]{2,1,0:T(8,128)(2,1)}, u32[]{:S(2)}, u32[]{:S(2)}) async-start(bf16[8,128,1024]{2,1,0:T(8,128)(2,1)} %gather_fusion.6), calls=%async_computation.2 | async-start | bytes 4194304 | tf_op jit(solution)/shard_map/all_to_all | solution.py:107
  79.7 68.6 %all-to-all-start = ((bf16[16,64,2048]{2,1,0:T(8,128)(2,1)}), bf16[16,64,2048]{2,1,0:T(8,128)(2,1)}, u32[]{:S(2)}, u32[]{:S(2)}) async-start(bf16[16,64,2048]{2,1,0:T(8,128)(2,1)} %select_select_fusion), calls=%async_computation | async-start | bytes 8388608 | tf_op jit(solution)/shard_map/all_to_all | solution.py:93
  157.0 10.3 %copy-start.4 = (bf16[1024,1024]{1,0:T(8,128)(2,1)S(1)}, bf16[1024,1024]{1,0:T(8,128)(2,1)}, u32[]{:S(2)}) copy-start(bf16[1024,1024]{1,0:T(8,128)(2,1)} %gather_fusion.5) | copy-start | bytes 6291460
  161.1 32.7 %all-to-all-start.3 = ((bf16[8,128,1024]{2,1,0:T(8,128)(2,1)}), bf16[8,128,1024]{2,1,0:T(8,128)(2,1)}, u32[]{:S(2)}, u32[]{:S(2)}) async-start(bf16[8,128,1024]{2,1,0:T(8,128)(2,1)} %copy.53), calls=%async_computation.3 | async-start | bytes 4194304 | tf_op jit(solution)/shard_map/all_to_all | solution.py:111
  167.4 8.5 %copy-start.6 = (bf16[1024,2048]{1,0:T(8,128)(2,1)S(1)}, bf16[1024,2048]{1,0:T(8,128)(2,1)}, u32[]{:S(2)}) copy-start(bf16[1024,2048]{1,0:T(8,128)(2,1)} %multiply_convert_fusion.1) | copy-start | bytes 12582916
  175.9 2.0 copy-start.9
  180.9 3.8 %copy-start.13 = (s32[1,8]{1,0:T(1,128)S(1)}, s32[1,8]{1,0:T(1,128)}, u32[]{:S(2)}) copy-start(s32[1,8]{1,0:T(1,128)} %param.16) | copy-start | bytes 100
  196.1 2.2 %copy-start.10 = (bf16[1024,2048]{1,0:T(8,128)(2,1)S(1)}, bf16[1024,2048]{1,0:T(8,128)(2,1)}, u32[]{:S(2)}) copy-start(bf16[1024,2048]{1,0:T(8,128)(2,1)} %copy-done.9) | copy-start | bytes 12582916
  198.3 2.2 %copy-start.7 = (bf16[1024,2048]{1,0:T(8,128)(2,1)S(1)}, bf16[1024,2048]{1,0:T(8,128)(2,1)}, u32[]{:S(2)}) copy-start(bf16[1024,2048]{1,0:T(8,128)(2,1)} %multiply_convert_fusion.1) | copy-start | bytes 12582916
  199.5 1.9 copy-start.5
  199.5 2.5 %copy-start.12 = (bf16[1024,1024]{1,0:T(8,128)(2,1)S(1)}, bf16[1024,1024]{1,0:T(8,128)(2,1)}, u32[]{:S(2)}) copy-start(bf16[1024,1024]{1,0:T(8,128)(2,1)} %param.21) | copy-start | bytes 6291460
  202.0 9.5 %copy-start.1 = (bf16[1024,1024]{1,0:T(8,128)(2,1)S(1)}, bf16[1024,1024]{1,0:T(8,128)(2,1)}, u32[]{:S(2)}) copy-start(bf16[1024,1024]{1,0:T(8,128)(2,1)} %param.18) | copy-start | bytes 6291460
where the time goes:
time: 213 us; the launch traced here: 211 us
  waiting for transfers between devices  78.2 us (37%)
  local copies, waits for them, and re-layouts  47.7 us (22%)
  matrix products  32.5 us (15%)
  other arithmetic  27.4 us (13%)
  starting transfers between devices  24.7 us (12%)
    all_to_all x1, waiting for transfers between devices, body(): lax.all_to_all(outgoing, 'cache', split_axis=0, concat_axis=0, tiled=True)  57.7 us
    dot_general x3, matrix products, silu_proj(): jnp.dot(normed, weight, preferred_element_type=jnp.float32)  23.2 us
    unnamed x31, local copies, waits for them, and re-layouts  13 us
    all_to_all x1, waiting for transfers between devices, body(): lax.all_to_all(send_queries, 'req', split_axis=0, concat_axis=0, tiled=True)  11.4 us
    all_to_all x1, waiting for transfers between devices, body(): lax.all_to_all(answer, 'req', split_axis=0, concat_axis=0, tiled=True)  9.1 us
    all_to_all x1, starting transfers between devices, body(): lax.all_to_all(slot_rows, 'req', split_axis=0, concat_axis=0, tiled=True)  6.81 us
    all_to_all x1, starting transfers between devices, body(): lax.all_to_all(outgoing, 'cache', split_axis=0, concat_axis=0, tiled=True)  6.8 us
    all_to_all x1, starting transfers between devices, body(): lax.all_to_all(answer, 'req', split_axis=0, concat_axis=0, tiled=True)  6.26 us
  transfers between devices with their start and end apart: 4, of which 3 were waited for; matrix products, arithmetic and copies ran while one was open for 34% of the time, Pallas kernels for 0%

commit v1 on v0

v1 whole, which is shorter than its diff:
```python
import jax
import jax.numpy as jnp
from jax import lax
from jax.experimental import pallas as pl
from jax.experimental.pallas import tpu as pltpu
from jax.sharding import PartitionSpec as P

D = 1024
HEADS = 8
HEAD_DIM = 128
HIST = 64
CB = 128
USERS = 16
REQS = 8
ROWS = 512
LIVE = 512
CHUNK = 16
CHUNKS = HIST // CHUNK
SCALE = HEAD_DIM ** (-0.5)
MESH = pl.DeviceIdType.MESH
F32 = jnp.float32
BF16 = jnp.bfloat16
I32 = jnp.int32

XY = [(2, 2), (0, 2), (2, 0), (3, 1), (1, 3), (3, 3), (1, 1), (2, 3), (3, 2), (2, 1), (1, 2), (3, 0), (0, 3), (1, 0), (0, 1)]
ZK = [(2, 0), (2, 1), (1, 0), (3, 0), (1, 1), (3, 1), (0, 1)]


def iota(shape, dim):
    return lax.broadcasted_iota(I32, shape, dim)


def silu(x):
    half = 0.5 * x
    return half + half * jnp.tanh(half)


def norm(x):
    mean = jnp.sum(x, axis=-1, keepdims=True) * (1.0 / D)
    centred = x - mean
    spread = jnp.sum(centred * centred, axis=-1, keepdims=True) * (1.0 / D)
    return centred * lax.rsqrt(spread + 1e-06)


def dot(a, b):
    return jnp.dot(a, b, preferred_element_type=F32)


def dot_nt(a, b):
    return lax.dot_general(a, b, (((1,), (1,)), ((), ())), preferred_element_type=F32)


def loop(n, body):
    def step(i, carry):
        body(i)
        return carry

    lax.fori_loop(0, n, step, 0)


def cols(i, width):
    return pl.ds(pl.multiple_of(i * width, width), width)


def request_bounds(counts):
    lane = iota((1, REQS), 1)
    starts = [jnp.sum(jnp.where(lane < j, counts, 0.0), axis=1, keepdims=True) for j in range(REQS)]
    lengths = [jnp.sum(jnp.where(lane == j, counts, 0.0), axis=1, keepdims=True) for j in range(REQS)]
    return starts, lengths


def exchange_kernel(
    feats_h, len_h, own_h, ids_h, count_h, rown_h, rslot_h, table_h, wqu_h, wkv_h,
    cache_h, gated_h, emb_h,
    feats, len_v, own_v, ids_v, count_v, rown_v, rslot_v, table, wqu, wkv,
    hn, pick, send, recv0, recv1, recv2, recv3, slot_out, slot_in, select,
    stage, back0, back1, back2, back3, kv, kvr,
    onehot, emb, cn, query, gate, skv, att, mask, gated,
    load_sem, ss1, rs1, ss2, rs2, sss, rss, out_sem, emb_sem, gated_sem,
):
    r = lax.axis_index("req")
    c = lax.axis_index("cache")
    z, k = r // 2, lax.rem(r, 2)
    y, x = c // 4, lax.rem(c, 4)
    recv = [recv0, recv1, recv2, recv3]
    back = [back0, back1, back2, back3]

    def plane(offset):
        dy, dx = offset
        return lax.rem(y + dy, 4) * 4 + lax.rem(x + dx, 4)

    def column(offset):
        dz, dk = offset
        return lax.rem(z + dz, 4) * 2 + lax.rem(k + dk, 2)

    barrier = pltpu.get_barrier_semaphore()
    for offset in XY:
        pl.semaphore_signal(barrier, inc=1, device_id=(r, plane(offset)), device_id_type=MESH)
    for offset in ZK:
        pl.semaphore_signal(barrier, inc=1, device_id=(column(offset), c), device_id_type=MESH)

    pairs = [
        (len_h, len_v), (own_h, own_v), (feats_h, feats), (count_h, count_v), (ids_h, ids_v), (rown_h, rown_v), (rslot_h, rslot_v),
        (table_h, table), (wqu_h, wqu), (wkv_h, wkv),
    ]
    loads = [pltpu.make_async_copy(src, dst, load_sem.at[i]) for i, (src, dst) in enumerate(pairs)]
    for copy in loads:
        copy.start()

    loads[0].wait()
    loads[1].wait()
    lengths = len_v[...].astype(F32)
    owner = own_v[...]
    lane_j = iota((USERS, USERS), 1)
    mine = owner == iota((USERS, USERS), 0)
    order = jnp.sum(jnp.where(mine, lane_j.astype(F32), 0.0), axis=1, keepdims=True)
    length_of = jnp.sum(jnp.where(mine, lengths, 0.0), axis=1, keepdims=True)
    start_of = jnp.sum(jnp.where(lane_j.astype(F32) < order, lengths, 0.0), axis=1, keepdims=True)
    row = iota((CHUNK, ROWS), 1).astype(F32)
    step_t = iota((CHUNK, ROWS), 0).astype(F32)
    for o in range(USERS):
        place = row - start_of[o : o + 1, :]
        live = place < length_of[o : o + 1, :]
        for q in range(CHUNKS):
            hit = jnp.logical_and(place == step_t + float(q * CHUNK), live)
            pick[q, o * CHUNK : (o + 1) * CHUNK, :] = jnp.where(hit, 1.0, 0.0).astype(BF16)

    loads[2].wait()

    def norm_feats(i):
        rows = cols(i, 64)
        hn[rows, :] = norm(feats[rows, :].astype(F32)).astype(BF16)

    loop(ROWS // 64, norm_feats)

    def slot_copy(i):
        to = column(ZK[i])
        return pltpu.make_async_remote_copy(
            src_ref=slot_out.at[to], dst_ref=slot_in.at[r], send_sem=sss.at[i], recv_sem=rss.at[i],
            device_id=(to, c), device_id_type=MESH,
        )

    def plane_copy(q, i):
        to = plane(XY[i])
        return pltpu.make_async_remote_copy(
            src_ref=send.at[q, cols(to, CHUNK), :], dst_ref=recv[q].at[cols(c, CHUNK), :],
            send_sem=ss1.at[q, i], recv_sem=rs1.at[q, i], device_id=(r, to), device_id_type=MESH,
        )

    def column_copy(q, i):
        to = column(ZK[i])
        return pltpu.make_async_remote_copy(
            src_ref=stage.at[q, cols(to, CHUNK), :], dst_ref=back[q].at[cols(r, CHUNK), :],
            send_sem=ss2.at[q, i], recv_sem=rs2.at[q, i], device_id=(to, c), device_id_type=MESH,
        )

    for q in range(CHUNKS):
        for n in range(2):
            send[q, :, n * 512 : (n + 1) * 512] = dot(pick[q], hn[:, n * 512 : (n + 1) * 512]).astype(BF16)
        if q == 0:
            pl.semaphore_wait(barrier, len(XY) + len(ZK))
        for i in range(len(XY)):
            plane_copy(q, i).start()
        recv[q][cols(c, CHUNK), :] = send[q, cols(c, CHUNK), :]

    for i in (3, 4, 5, 6):
        loads[i].wait()
    req_owner = rown_v[...]
    req_slot = rslot_v[...]
    for o in range(REQS):
        wanted = jnp.sum(jnp.where(req_owner == o, req_slot.astype(F32), 0.0), axis=1, keepdims=True)
        slot_out[o] = jnp.broadcast_to(wanted, (8, 128)).astype(I32)
    for i in range(len(ZK)):
        slot_copy(i).start()
    slot_in[r] = slot_out[r]

    starts, counts = request_bounds(count_v[...].astype(F32))
    packed = iota((LIVE, CB), 0).astype(F32)
    lane = iota((LIVE, CB), 1).astype(F32)
    lane_owner = iota((LIVE, CB), 1) // CHUNK
    id_sum = jnp.zeros((LIVE, CB), F32)
    owner_sum = jnp.zeros((LIVE, CB), F32)
    req_owner_f = req_owner.astype(F32)
    for j in range(REQS):
        place = packed - starts[j]
        hit = jnp.logical_and(place == lane, lane < counts[j])
        id_sum = id_sum + jnp.where(hit, ids_v[0:1, j * CB : (j + 1) * CB].astype(F32), 0.0)
        inside = jnp.logical_and(place >= 0.0, place < counts[j])
        owner_sum = owner_sum + jnp.where(inside, req_owner_f[:, j : j + 1], 0.0)
    mask[...] = jnp.where(owner_sum == lane_owner.astype(F32), 1.0, 0.0)
    ids = jnp.sum(id_sum, axis=1, keepdims=True)
    for n in range(D // 128):
        word = (iota((LIVE, 128), 1) + n * 128).astype(F32)
        onehot[:, n * 128 : (n + 1) * 128] = jnp.where(ids == word, 1.0, 0.0).astype(BF16)

    loads[7].wait()

    def embed(n):
        emb[:, cols(n, 256)] = dot(onehot[...], table[:, cols(n, 256)]).astype(BF16)

    loop(D // 256, embed)
    emb_copy = pltpu.make_async_copy(emb, emb_h, emb_sem)
    emb_copy.start()

    def norm_emb(i):
        rows = cols(i, 64)
        cn[rows, :] = norm(emb[rows, :].astype(F32)).astype(BF16)

    loop(LIVE // 64, norm_emb)
    loads[8].wait()

    def project_q(n):
        query[:, cols(n, 256)] = silu(dot(cn[...], wqu[:, cols(n, 256)])).astype(BF16)
        gate[:, cols(n, 256)] = silu(dot(cn[...], wqu[:, pl.ds(pl.multiple_of(D + n * 256, 256), 256)])).astype(BF16)

    loop(D // 256, project_q)
    loads[9].wait()

    def project_kv(n):
        skv[:, cols(n, 256)] = silu(dot(cn[...], wkv[:, cols(n, 256)])).astype(BF16)

    loop(2 * D // 256, project_kv)

    def self_attend(h):
        head = cols(h, HEAD_DIM)
        product = query[:, head].astype(F32) * skv[:, head].astype(F32)
        weight = silu(jnp.sum(product, axis=1, keepdims=True) * SCALE)
        value = skv[:, pl.ds(pl.multiple_of(D + h * HEAD_DIM, HEAD_DIM), HEAD_DIM)].astype(F32)
        att[:, head] = weight * value

    loop(HEADS, self_attend)

    for i in range(len(ZK)):
        slot_copy(i).wait_recv()
    lane_row = iota((CHUNK, USERS * CHUNK), 1).astype(F32)
    step_s = iota((CHUNK, USERS * CHUNK), 0).astype(F32)
    for o in range(REQS):
        slot = slot_in[o][0:1, 0:1].astype(F32)
        hit = lane_row == slot * float(CHUNK) + step_s
        select[o * CHUNK : (o + 1) * CHUNK, :] = jnp.where(hit, 1.0, 0.0).astype(BF16)

    def attend_chunk(q):
        for i in range(len(ZK)):
            column_copy(q, i).wait_recv()

        def project(n):
            kvr[:, cols(n, 512)] = silu(dot(back[q][...], wkv[:, cols(n, 512)])).astype(BF16)

        loop(2 * D // 512, project)

        def attend(h):
            head = cols(h, HEAD_DIM)
            weight = silu(dot_nt(query[:, head], kvr[:, head]) * SCALE) * mask[...]
            value = kvr[:, pl.ds(pl.multiple_of(D + h * HEAD_DIM, HEAD_DIM), HEAD_DIM)]
            att[:, head] += dot(weight.astype(BF16), value)

        loop(HEADS, attend)

    for q in range(CHUNKS):
        for i in range(len(XY)):
            plane_copy(q, i).wait_recv()
        for n in range(2):
            stage[q, :, n * 512 : (n + 1) * 512] = dot(select[...], recv[q][:, n * 512 : (n + 1) * 512]).astype(BF16)
        for i in range(len(ZK)):
            column_copy(q, i).start()
        back[q][cols(r, CHUNK), :] = stage[q, cols(r, CHUNK), :]

        def project(n, q=q):
            block = silu(dot(recv[q][...], wkv[:, cols(n, 256)])).astype(BF16)
            kv[q, :, :, cols(n, 256)] = block.reshape(USERS, CHUNK, 256)

        loop(2 * D // 256, project)
        pltpu.make_async_copy(kv.at[q], cache_h.at[:, pl.ds(q * CHUNK, CHUNK), :], out_sem.at[q]).start()
        attend_chunk(q)

    def finish(i):
        rows = cols(i, 64)
        gated[rows, :] = (norm(att[rows, :]) * gate[rows, :].astype(F32)).astype(BF16)

    loop(LIVE // 64, finish)
    gated_copy = pltpu.make_async_copy(gated, gated_h, gated_sem)
    gated_copy.start()
    for i in range(len(ZK)):
        slot_copy(i).wait_send()
    for q in range(CHUNKS):
        for i in range(len(XY)):
            plane_copy(q, i).wait_send()
        for i in range(len(ZK)):
            column_copy(q, i).wait_send()
        pltpu.make_async_copy(kv.at[q], cache_h.at[:, pl.ds(q * CHUNK, CHUNK), :], out_sem.at[q]).wait()
    emb_copy.wait()
    gated_copy.wait()


def exchange(feats, lens, owners, ids, counts, req_owner, req_slot, table, w_qu, w_kv):
    any_spec = pl.BlockSpec(memory_space=pl.ANY)
    vmem = pltpu.VMEM
    return pl.pallas_call(
        exchange_kernel,
        out_shape=(
            jax.ShapeDtypeStruct((USERS, HIST, 2 * D), BF16),
            jax.ShapeDtypeStruct((LIVE, D), BF16),
            jax.ShapeDtypeStruct((LIVE, D), BF16),
        ),
        in_specs=[any_spec] * 10,
        out_specs=(any_spec,) * 3,
        scratch_shapes=[
            vmem((ROWS, D), BF16),
            vmem((1, USERS), I32), vmem((1, USERS), I32), vmem((1, REQS * CB), I32), vmem((1, REQS), I32),
            vmem((1, REQS), I32), vmem((1, REQS), I32),
            vmem((D, D), BF16), vmem((D, 2 * D), BF16), vmem((D, 2 * D), BF16),
            vmem((ROWS, D), BF16),
            vmem((CHUNKS, USERS * CHUNK, ROWS), BF16),
            vmem((CHUNKS, USERS * CHUNK, D), BF16),
        ]
        + [vmem((USERS * CHUNK, D), BF16)] * CHUNKS
        + [
            vmem((REQS, 8, 128), I32), vmem((REQS, 8, 128), I32),
            vmem((REQS * CHUNK, USERS * CHUNK), BF16),
            vmem((CHUNKS, REQS * CHUNK, D), BF16),
        ]
        + [vmem((REQS * CHUNK, D), BF16)] * CHUNKS
        + [
            vmem((CHUNKS, USERS, CHUNK, 2 * D), BF16),
            vmem((REQS * CHUNK, 2 * D), BF16),
            vmem((LIVE, D), BF16), vmem((LIVE, D), BF16), vmem((LIVE, D), BF16),
            vmem((LIVE, D), BF16), vmem((LIVE, D), BF16), vmem((LIVE, 2 * D), BF16),
            vmem((LIVE, D), F32), vmem((LIVE, CB), F32), vmem((LIVE, D), BF16),
            pltpu.SemaphoreType.DMA((10,)),
            pltpu.SemaphoreType.DMA((CHUNKS, len(XY))), pltpu.SemaphoreType.DMA((CHUNKS, len(XY))),
            pltpu.SemaphoreType.DMA((CHUNKS, len(ZK))), pltpu.SemaphoreType.DMA((CHUNKS, len(ZK))),
            pltpu.SemaphoreType.DMA((len(ZK),)), pltpu.SemaphoreType.DMA((len(ZK),)),
            pltpu.SemaphoreType.DMA((CHUNKS,)), pltpu.SemaphoreType.DMA, pltpu.SemaphoreType.DMA,
        ],
        compiler_params=pltpu.CompilerParams(collective_id=0, has_side_effects=True, vmem_limit_bytes=52 << 20),
        cost_estimate=pl.CostEstimate(flops=13 << 30, bytes_accessed=20 << 20, transcendentals=8 << 20),
        name="exchange",
    )(feats, lens, owners, ids, counts, req_owner, req_slot, table, w_qu, w_kv)


def output_kernel(cache_in, gated_h, emb_h, wout_h, count_h, cache_out, cand_h, gated, emb, wout, count_v, res, pick, out, sem, cache_sem, out_sem):
    pairs = [(count_h, count_v), (gated_h, gated), (wout_h, wout), (emb_h, emb)]
    loads = [pltpu.make_async_copy(src, dst, sem.at[i]) for i, (src, dst) in enumerate(pairs)]
    for copy in loads:
        copy.start()
    moves = [
        pltpu.make_async_copy(cache_in.at[pl.ds(i * 4, 4)], cache_out.at[pl.ds(i * 4, 4)], cache_sem.at[i]) for i in range(4)
    ]
    for copy in moves:
        copy.start()
    loads[0].wait()
    starts, counts = request_bounds(count_v[...].astype(F32))
    packed = iota((CB, LIVE), 1).astype(F32)
    slot = iota((CB, LIVE), 0).astype(F32)
    for j in range(REQS):
        hit = jnp.logical_and(packed - starts[j] == slot, slot < counts[j])
        pick[j * CB : (j + 1) * CB, :] = jnp.where(hit, 1.0, 0.0).astype(BF16)
    for i in (1, 2, 3):
        loads[i].wait()

    def project(n):
        res[:, cols(n, 256)] = (dot(gated[...], wout[:, cols(n, 256)]) + emb[:, cols(n, 256)].astype(F32)).astype(BF16)

    loop(D // 256, project)

    def out_copy(j):
        rows = pl.ds(j * 256, 256)
        return pltpu.make_async_copy(out.at[rows], cand_h.at[rows], out_sem.at[j])

    for j in range(4):
        rows = slice(j * 256, (j + 1) * 256)
        for n in range(2):
            out[rows, n * 512 : (n + 1) * 512] = dot(pick[rows, :], res[:, n * 512 : (n + 1) * 512]).astype(BF16)
        out_copy(j).start()
    for j in range(4):
        out_copy(j).wait()
    for copy in moves:
        copy.wait()


def output(cache, gated, emb, w_out, counts):
    any_spec = pl.BlockSpec(memory_space=pl.ANY)
    vmem = pltpu.VMEM
    return pl.pallas_call(
        output_kernel,
        out_shape=(
            jax.ShapeDtypeStruct((USERS, HIST, 2 * D), BF16),
            jax.ShapeDtypeStruct((REQS * CB, D), BF16),
        ),
        in_specs=[any_spec] * 5,
        out_specs=(any_spec,) * 2,
        scratch_shapes=[
            vmem((LIVE, D), BF16), vmem((LIVE, D), BF16), vmem((D, D), BF16), vmem((1, REQS), I32),
            vmem((LIVE, D), BF16), vmem((REQS * CB, LIVE), BF16), vmem((REQS * CB, D), BF16),
            pltpu.SemaphoreType.DMA((4,)), pltpu.SemaphoreType.DMA((4,)), pltpu.SemaphoreType.DMA((4,)),
        ],
        compiler_params=pltpu.CompilerParams(vmem_limit_bytes=24 << 20),
        cost_estimate=pl.CostEstimate(flops=2 << 30, bytes_accessed=16 << 20, transcendentals=0),
        name="output",
    )(cache, gated, emb, w_out, counts)


def body(event_feats, hist_len, user_owner, cand_ids, cand_count, req_owner, req_slot, table, w_qu, w_kv, w_out):
    cache, gated, emb = exchange(
        event_feats[0], hist_len, user_owner, cand_ids, cand_count, req_owner, req_slot, table, w_qu, w_kv
    )
    cache, cand_out = output(cache, gated, emb, w_out, cand_count)
    return (cache[None], cand_out[None])


def solution(mesh):
    in_specs = (
        P(("req", "cache"), None, None),
        P(("req", "cache"), None),
        P(("req", "cache"), None),
        P(("req", "cache"), None),
        P(("req", "cache"), None),
        P(("req", "cache"), None),
        P(("req", "cache"), None),
        P(),
        P(),
        P(),
        P(),
    )
    out_specs = (P(("req", "cache"), None, None, None), P(("req", "cache"), None, None))
    return jax.shard_map(body, mesh=mesh, in_specs=in_specs, out_specs=out_specs, check_vma=False)
```

time: 213 us -> 77 us (0.36)
  waiting for transfers between devices: 78.2 us -> 0 us
  Pallas kernels: 0 us -> 68.7 us
  local copies, waits for them, and re-layouts: 47.7 us -> 7.36 us
  matrix products: 32.5 us -> 0 us
  other arithmetic: 27.4 us -> 0 us
  starting transfers between devices: 24.7 us -> 0 us
    all_to_all x4 -> x0, waiting for transfers between devices: 78.2 us -> none  [the longest x1 57.7 us: body(): lax.all_to_all(outgoing, 'cache', split_axis=0, concat_axis=0, tiled=True)]
    pallas_call x0 -> x2, Pallas kernels: none -> 68.7 us  [the longest x1 64.1 us: exchange(): pl.pallas_call(exchange_kernel, out_shape=(jax.ShapeDtypeStruct((USERS, H...]
    dot_general x5 -> x0, matrix products: 32.5 us -> none  [the longest x3 23.2 us: silu_proj(): jnp.dot(normed, weight, preferred_element_type=jnp.float32)]
    all_to_all x4 -> x0, starting transfers between devices: 24.7 us -> none  [the longest x1 6.81 us: body(): lax.all_to_all(slot_rows, 'req', split_axis=0, concat_axis=0, tiled=True)]
    gather x9 -> x0, local copies, waits for them, and re-layouts: 22.7 us -> none  [the longest x1 5.96 us: body(): jnp.take(packed_kv, row_index, axis=0)]
    reduce_sum x7 -> x0, other arithmetic: 12.8 us -> none  [the longest x3 4.83 us: layer_norm(): mean = jnp.mean(values, axis=-1, keepdims=True)]
    unnamed x31 -> x18, local copies, waits for them, and re-layouts: 13 us -> 7.36 us
    select_n x7 -> x0, other arithmetic: 4.72 us -> none  [the longest x1 3.94 us: body(): jnp.where(live_mask[..., None], jnp.take(packed_kv, row_index, axis=0), z...]
  transfers between devices with their start and end apart: 4 -> 0, of which waited for: 3 -> 0; matrix products, arithmetic and copies ran while one was open for 34% -> 0% of each run, Pallas kernels for 0% -> 0%
where the time goes in v1:
time: 77 us; the launch traced here: 76.7 us
  Pallas kernels  68.7 us (89%)
  local copies, waits for them, and re-layouts  7.36 us (10%)
    pallas_call x1, Pallas kernels, exchange(): pl.pallas_call(exchange_kernel, out_shape=(jax.ShapeDtypeStruct((USERS, H...  64.1 us
    unnamed x18, local copies, waits for them, and re-layouts  7.36 us
    pallas_call x1, Pallas kernels, output(): pl.pallas_call(output_kernel, out_shape=(jax.ShapeDtypeStruct((USERS, HIS...  4.59 us

profile of v1, /device:TPU:1, one launch (start us, length us, event | category | flops | bytes accessed | tf_op | source)
XLA Modules:
  0.0 76.7 jit_solution(8162037824034826482)
XLA Ops:
  0.6 0.0 copy-start.3
  0.6 0.6 copy-done.3
  1.3 0.0 copy-start.4
  1.3 0.7 copy-done.4
  2.0 0.0 copy-start.5
  2.0 0.7 copy-done.5
  2.6 0.0 copy-start.6
  2.6 0.7 copy-done.6
  3.3 0.0 copy-start.7
  3.3 0.7 copy-done.7
  3.9 0.0 copy-start.8
  3.9 0.7 copy-done.8
  4.6 0.0 copy-start.1
  4.6 64.1 %exchange.1 = (bf16[16,64,2048]{2,1,0:T(8,128)(2,1)}, bf16[512,1024]{1,0:T(8,128)(2,1)S(1)}, bf16[512,1024]{1,0:T(8,128)(2,1)}) custom-call(bf16[512,1024]{1,0:T(8,128)(2,1)} %bitcast.5, s32[1,16]{1,0:T(1,128)S(1)} %copy-done.5, s32[1,16]{1,0:T(1,128)S(1)} %copy-done.6, s32[1,1024]{1,0:T(1,128)S(1)} %copy-done.4, s32[1,8]{1,0:T(1,128)S(1)} %copy-done.3, ...), custom_call_target="tpu_custom_call" | custom-call | flops 13958643712 | bytes 20971520 | tf_op jit(solution)/shard_map/exchange/pallas_call | solution.py:298
  68.7 0.0 copy-done.1
  68.7 0.0 copy-start
  68.7 2.2 %copy-done = bf16[16,64,2048]{2,1,0:T(8,128)(2,1)S(1)} copy-done((bf16[16,64,2048]{2,1,0:T(8,128)(2,1)S(1)}, bf16[16,64,2048]{2,1,0:T(8,128)(2,1)}, u32[]{:S(2)}) %copy-start) | copy-done | bytes 4194328
  70.9 0.0 copy-start.2
  70.9 1.2 %copy-done.2 = bf16[512,1024]{1,0:T(8,128)(2,1)S(1)} copy-done((bf16[512,1024]{1,0:T(8,128)(2,1)S(1)}, bf16[512,1024]{1,0:T(8,128)(2,1)}, u32[]{:S(2)}) %copy-start.2) | copy-done | bytes 1048600
  72.1 4.6 %output.1 = (bf16[16,64,2048]{2,1,0:T(8,128)(2,1)}, bf16[1024,1024]{1,0:T(8,128)(2,1)}) custom-call(bf16[16,64,2048]{2,1,0:T(8,128)(2,1)S(1)} %copy-done, bf16[512,1024]{1,0:T(8,128)(2,1)S(1)} %get-tuple-element.8.gated_h, bf16[512,1024]{1,0:T(8,128)(2,1)S(1)} %copy-done.2, bf16[1024,1024]{1,0:T(8,128)(2,1)S(1)} %copy-done.1, s32[1,8]{1,0:T(1,128)S(1)} %copy-done.3), custom_call_target="tpu_custom_call" | custom-call | flops 2147483648 | bytes 16777216 | tf_op jit(solution)/shard_map/output/pallas_call | solution.py:384
Async XLA Ops:
  0.6 0.7 copy-start.3
  1.3 0.7 copy-start.4
  2.0 0.7 copy-start.5
  2.6 0.7 copy-start.6
  3.3 0.7 copy-start.7
  3.9 0.7 copy-start.8
  4.6 64.1 %copy-start.1 = (bf16[1024,1024]{1,0:T(8,128)(2,1)S(1)}, bf16[1024,1024]{1,0:T(8,128)(2,1)}, u32[]{:S(2)}) copy-start(bf16[1024,1024]{1,0:T(8,128)(2,1)} %wout_h.1) | copy-start | bytes 6291460
  68.7 2.2 %copy-start = (bf16[16,64,2048]{2,1,0:T(8,128)(2,1)S(1)}, bf16[16,64,2048]{2,1,0:T(8,128)(2,1)}, u32[]{:S(2)}) copy-start(bf16[16,64,2048]{2,1,0:T(8,128)(2,1)} %get-tuple-element.7.cache_in) | copy-start | bytes 12582916
  70.9 1.2 %copy-start.2 = (bf16[512,1024]{1,0:T(8,128)(2,1)S(1)}, bf16[512,1024]{1,0:T(8,128)(2,1)}, u32[]{:S(2)}) copy-start(bf16[512,1024]{1,0:T(8,128)(2,1)} %get-tuple-element.9.emb_h) | copy-start | bytes 3145732

commit v2 on v1

--- a/solution.py
+++ b/solution.py
@@ -26,6 +26,10 @@
 ZK = [(2, 0), (2, 1), (1, 0), (3, 0), (1, 1), (3, 1), (0, 1)]
 
 
+def in_hbm(array):
+    return pltpu.with_memory_space_constraint(array, pltpu.HBM)
+
+
 def iota(shape, dim):
     return lax.broadcasted_iota(I32, shape, dim)
 
@@ -50,14 +54,6 @@
     return lax.dot_general(a, b, (((1,), (1,)), ((), ())), preferred_element_type=F32)
 
 
-def loop(n, body):
-    def step(i, carry):
-        body(i)
-        return carry
-
-    lax.fori_loop(0, n, step, 0)
-
-
 def cols(i, width):
     return pl.ds(pl.multiple_of(i * width, width), width)
 
@@ -71,12 +67,12 @@
 
 def exchange_kernel(
     feats_h, len_h, own_h, ids_h, count_h, rown_h, rslot_h, table_h, wqu_h, wkv_h,
-    cache_h, gated_h, emb_h,
+    kv, gated, emb,
     feats, len_v, own_v, ids_v, count_v, rown_v, rslot_v, table, wqu, wkv,
     hn, pick, send, recv0, recv1, recv2, recv3, slot_out, slot_in, select,
-    stage, back0, back1, back2, back3, kv, kvr,
-    onehot, emb, cn, query, gate, skv, att, mask, gated,
-    load_sem, ss1, rs1, ss2, rs2, sss, rss, out_sem, emb_sem, gated_sem,
+    stage, back0, back1, back2, back3, kvr,
+    onehot, cn, query, gate, skv, att, mask,
+    load_sem, ss1, rs1, ss2, rs2, sss, rss,
 ):
     r = lax.axis_index("req")
     c = lax.axis_index("cache")
@@ -127,11 +123,9 @@
 
     loads[2].wait()
 
-    def norm_feats(i):
-        rows = cols(i, 64)
+    for i in range(ROWS // 64):
+        rows = slice(i * 64, (i + 1) * 64)
         hn[rows, :] = norm(feats[rows, :].astype(F32)).astype(BF16)
-
-    loop(ROWS // 64, norm_feats)
 
     def slot_copy(i):
         to = column(ZK[i])
@@ -155,8 +149,7 @@
         )
 
     for q in range(CHUNKS):
-        for n in range(2):
-            send[q, :, n * 512 : (n + 1) * 512] = dot(pick[q], hn[:, n * 512 : (n + 1) * 512]).astype(BF16)
+        send[q] = dot(pick[q], hn[...]).astype(BF16)
         if q == 0:
             pl.semaphore_wait(barrier, len(XY) + len(ZK))
         for i in range(len(XY)):
@@ -195,40 +188,21 @@
 
     loads[7].wait()
 
-    def embed(n):
-        emb[:, cols(n, 256)] = dot(onehot[...], table[:, cols(n, 256)]).astype(BF16)
-
-    loop(D // 256, embed)
-    emb_copy = pltpu.make_async_copy(emb, emb_h, emb_sem)
-    emb_copy.start()
-
-    def norm_emb(i):
-        rows = cols(i, 64)
+    emb[...] = dot(onehot[...], table[...]).astype(BF16)
+    for i in range(LIVE // 64):
+        rows = slice(i * 64, (i + 1) * 64)
         cn[rows, :] = norm(emb[rows, :].astype(F32)).astype(BF16)
-
-    loop(LIVE // 64, norm_emb)
     loads[8].wait()
-
-    def project_q(n):
-        query[:, cols(n, 256)] = silu(dot(cn[...], wqu[:, cols(n, 256)])).astype(BF16)
-        gate[:, cols(n, 256)] = silu(dot(cn[...], wqu[:, pl.ds(pl.multiple_of(D + n * 256, 256), 256)])).astype(BF16)
-
-    loop(D // 256, project_q)
+    query[...] = silu(dot(cn[...], wqu[:, :D])).astype(BF16)
+    gate[...] = silu(dot(cn[...], wqu[:, D:])).astype(BF16)
     loads[9].wait()
-
-    def project_kv(n):
-        skv[:, cols(n, 256)] = silu(dot(cn[...], wkv[:, cols(n, 256)])).astype(BF16)
-
-    loop(2 * D // 256, project_kv)
-
-    def self_attend(h):
-        head = cols(h, HEAD_DIM)
+    skv[...] = silu(dot(cn[...], wkv[...])).astype(BF16)
+    for h in range(HEADS):
+        head = slice(h * HEAD_DIM, (h + 1) * HEAD_DIM)
+        value = slice(D + h * HEAD_DIM, D + (h + 1) * HEAD_DIM)
         product = query[:, head].astype(F32) * skv[:, head].astype(F32)
         weight = silu(jnp.sum(product, axis=1, keepdims=True) * SCALE)
-        value = skv[:, pl.ds(pl.multiple_of(D + h * HEAD_DIM, HEAD_DIM), HEAD_DIM)].astype(F32)
-        att[:, head] = weight * value
-
-    loop(HEADS, self_attend)
+        att[:, head] = weight * skv[:, value].astype(F32)
 
     for i in range(len(ZK)):
         slot_copy(i).wait_recv()
@@ -242,44 +216,29 @@
     def attend_chunk(q):
         for i in range(len(ZK)):
             column_copy(q, i).wait_recv()
-
-        def project(n):
-            kvr[:, cols(n, 512)] = silu(dot(back[q][...], wkv[:, cols(n, 512)])).astype(BF16)
-
-        loop(2 * D // 512, project)
-
-        def attend(h):
-            head = cols(h, HEAD_DIM)
+        kvr[...] = silu(dot(back[q][...], wkv[...])).astype(BF16)
+        for h in range(HEADS):
+            head = slice(h * HEAD_DIM, (h + 1) * HEAD_DIM)
+            value = slice(D + h * HEAD_DIM, D + (h + 1) * HEAD_DIM)
             weight = silu(dot_nt(query[:, head], kvr[:, head]) * SCALE) * mask[...]
-            value = kvr[:, pl.ds(pl.multiple_of(D + h * HEAD_DIM, HEAD_DIM), HEAD_DIM)]
-            att[:, head] += dot(weight.astype(BF16), value)
-
-        loop(HEADS, attend)
+            att[:, head] += dot(weight.astype(BF16), kvr[:, value])
 
     for q in range(CHUNKS):
         for i in range(len(XY)):
             plane_copy(q, i).wait_recv()
-        for n in range(2):
-            stage[q, :, n * 512 : (n + 1) * 512] = dot(select[...], recv[q][:, n * 512 : (n + 1) * 512]).astype(BF16)
+        stage[q] = dot(select[...], recv[q][...]).astype(BF16)
         for i in range(len(ZK)):
             column_copy(q, i).start()
         back[q][cols(r, CHUNK), :] = stage[q, cols(r, CHUNK), :]
-
-        def project(n, q=q):
-            block = silu(dot(recv[q][...], wkv[:, cols(n, 256)])).astype(BF16)
-            kv[q, :, :, cols(n, 256)] = block.reshape(USERS, CHUNK, 256)
-
-        loop(2 * D // 256, project)
-        pltpu.make_async_copy(kv.at[q], cache_h.at[:, pl.ds(q * CHUNK, CHUNK), :], out_sem.at[q]).start()
-        attend_chunk(q)
-
-    def finish(i):
-        rows = cols(i, 64)
+        block = silu(dot(recv[q][...], wkv[...])).astype(BF16)
+        kv[:, q * CHUNK : (q + 1) * CHUNK, :] = block.reshape(USERS, CHUNK, 2 * D)
+        if q > 0:
+            attend_chunk(q - 1)
+    attend_chunk(CHUNKS - 1)
+
+    for i in range(LIVE // 64):
+        rows = slice(i * 64, (i + 1) * 64)
         gated[rows, :] = (norm(att[rows, :]) * gate[rows, :].astype(F32)).astype(BF16)
-
-    loop(LIVE // 64, finish)
-    gated_copy = pltpu.make_async_copy(gated, gated_h, gated_sem)
-    gated_copy.start()
     for i in range(len(ZK)):
         slot_copy(i).wait_send()
     for q in range(CHUNKS):
@@ -287,9 +246,6 @@
             plane_copy(q, i).wait_send()
         for i in range(len(ZK)):
             column_copy(q, i).wait_send()
-        pltpu.make_async_copy(kv.at[q], cache_h.at[:, pl.ds(q * CHUNK, CHUNK), :], out_sem.at[q]).wait()
-    emb_copy.wait()
-    gated_copy.wait()
 
 
 def exchange(feats, lens, owners, ids, counts, req_owner, req_slot, table, w_qu, w_kv):
@@ -298,12 +254,12 @@
     return pl.pallas_call(
         exchange_kernel,
         out_shape=(
-            jax.ShapeDtypeStruct((USERS, HIST, 2 * D), BF16),
-            jax.ShapeDtypeStruct((LIVE, D), BF16),
-            jax.ShapeDtypeStruct((LIVE, D), BF16),
+            pltpu.VMEM((USERS, HIST, 2 * D), BF16),
+            pltpu.VMEM((LIVE, D), BF16),
+            pltpu.VMEM((LIVE, D), BF16),
         ),
         in_specs=[any_spec] * 10,
-        out_specs=(any_spec,) * 3,
+        out_specs=(pl.BlockSpec(memory_space=pltpu.VMEM),) * 3,
         scratch_shapes=[
             vmem((ROWS, D), BF16),
             vmem((1, USERS), I32), vmem((1, USERS), I32), vmem((1, REQS * CB), I32), vmem((1, REQS), I32),
@@ -321,47 +277,37 @@
         ]
         + [vmem((REQS * CHUNK, D), BF16)] * CHUNKS
         + [
-            vmem((CHUNKS, USERS, CHUNK, 2 * D), BF16),
             vmem((REQS * CHUNK, 2 * D), BF16),
-            vmem((LIVE, D), BF16), vmem((LIVE, D), BF16), vmem((LIVE, D), BF16),
+            vmem((LIVE, D), BF16), vmem((LIVE, D), BF16),
             vmem((LIVE, D), BF16), vmem((LIVE, D), BF16), vmem((LIVE, 2 * D), BF16),
-            vmem((LIVE, D), F32), vmem((LIVE, CB), F32), vmem((LIVE, D), BF16),
+            vmem((LIVE, D), F32), vmem((LIVE, CB), F32),
             pltpu.SemaphoreType.DMA((10,)),
             pltpu.SemaphoreType.DMA((CHUNKS, len(XY))), pltpu.SemaphoreType.DMA((CHUNKS, len(XY))),
             pltpu.SemaphoreType.DMA((CHUNKS, len(ZK))), pltpu.SemaphoreType.DMA((CHUNKS, len(ZK))),
             pltpu.SemaphoreType.DMA((len(ZK),)), pltpu.SemaphoreType.DMA((len(ZK),)),
-            pltpu.SemaphoreType.DMA((CHUNKS,)), pltpu.SemaphoreType.DMA, pltpu.SemaphoreType.DMA,
         ],
-        compiler_params=pltpu.CompilerParams(collective_id=0, has_side_effects=True, vmem_limit_bytes=52 << 20),
+        compiler_params=pltpu.CompilerParams(collective_id=0, has_side_effects=True, vmem_limit_bytes=46 << 20),
         cost_estimate=pl.CostEstimate(flops=13 << 30, bytes_accessed=20 << 20, transcendentals=8 << 20),
         name="exchange",
     )(feats, lens, owners, ids, counts, req_owner, req_slot, table, w_qu, w_kv)
 
 
-def output_kernel(cache_in, gated_h, emb_h, wout_h, count_h, cache_out, cand_h, gated, emb, wout, count_v, res, pick, out, sem, cache_sem, out_sem):
-    pairs = [(count_h, count_v), (gated_h, gated), (wout_h, wout), (emb_h, emb)]
-    loads = [pltpu.make_async_copy(src, dst, sem.at[i]) for i, (src, dst) in enumerate(pairs)]
-    for copy in loads:
-        copy.start()
+def output_kernel(cache_in, gated, emb, wout, count_h, cache_out, cand_h, count_v, res, pick, out, sem, cache_sem, out_sem):
+    load = pltpu.make_async_copy(count_h, count_v, sem)
+    load.start()
     moves = [
         pltpu.make_async_copy(cache_in.at[pl.ds(i * 4, 4)], cache_out.at[pl.ds(i * 4, 4)], cache_sem.at[i]) for i in range(4)
     ]
     for copy in moves:
         copy.start()
-    loads[0].wait()
+    res[...] = (dot(gated[...], wout[...]) + emb[...].astype(F32)).astype(BF16)
+    load.wait()
     starts, counts = request_bounds(count_v[...].astype(F32))
     packed = iota((CB, LIVE), 1).astype(F32)
     slot = iota((CB, LIVE), 0).astype(F32)
     for j in range(REQS):
         hit = jnp.logical_and(packed - starts[j] == slot, slot < counts[j])
         pick[j * CB : (j + 1) * CB, :] = jnp.where(hit, 1.0, 0.0).astype(BF16)
-    for i in (1, 2, 3):
-        loads[i].wait()
-
-    def project(n):
-        res[:, cols(n, 256)] = (dot(gated[...], wout[:, cols(n, 256)]) + emb[:, cols(n, 256)].astype(F32)).astype(BF16)
-
-    loop(D // 256, project)
 
     def out_copy(j):
         rows = pl.ds(j * 256, 256)
@@ -369,8 +315,7 @@
 
     for j in range(4):
         rows = slice(j * 256, (j + 1) * 256)
-        for n in range(2):
-            out[rows, n * 512 : (n + 1) * 512] = dot(pick[rows, :], res[:, n * 512 : (n + 1) * 512]).astype(BF16)
+        out[rows, :] = dot(pick[rows, :], res[...]).astype(BF16)
         out_copy(j).start()
     for j in range(4):
         out_copy(j).wait()
@@ -387,22 +332,22 @@
             jax.ShapeDtypeStruct((USERS, HIST, 2 * D), BF16),
             jax.ShapeDtypeStruct((REQS * CB, D), BF16),
         ),
-        in_specs=[any_spec] * 5,
+        in_specs=[pl.BlockSpec(memory_space=vmem)] * 4 + [any_spec],
         out_specs=(any_spec,) * 2,
         scratch_shapes=[
-            vmem((LIVE, D), BF16), vmem((LIVE, D), BF16), vmem((D, D), BF16), vmem((1, REQS), I32),
+            vmem((1, REQS), I32),
             vmem((LIVE, D), BF16), vmem((REQS * CB, LIVE), BF16), vmem((REQS * CB, D), BF16),
-            pltpu.SemaphoreType.DMA((4,)), pltpu.SemaphoreType.DMA((4,)), pltpu.SemaphoreType.DMA((4,)),
+            pltpu.SemaphoreType.DMA, pltpu.SemaphoreType.DMA((4,)), pltpu.SemaphoreType.DMA((4,)),
         ],
         compiler_params=pltpu.CompilerParams(vmem_limit_bytes=24 << 20),
         cost_estimate=pl.CostEstimate(flops=2 << 30, bytes_accessed=16 << 20, transcendentals=0),
         name="output",
-    )(cache, gated, emb, w_out, counts)
+    )(cache, gated, emb, w_out, in_hbm(counts))
 
 
 def body(event_feats, hist_len, user_owner, cand_ids, cand_count, req_owner, req_slot, table, w_qu, w_kv, w_out):
     cache, gated, emb = exchange(
-        event_feats[0], hist_len, user_owner, cand_ids, cand_count, req_owner, req_slot, table, w_qu, w_kv
+        *(in_hbm(a) for a in (event_feats[0], hist_len, user_owner, cand_ids, cand_count, req_owner, req_slot, table, w_qu, w_kv))
     )
     cache, cand_out = output(cache, gated, emb, w_out, cand_count)
     return (cache[None], cand_out[None])

time: 77 us -> 47.7 us (0.62)
  Pallas kernels: 68.7 us -> 46.7 us
  local copies, waits for them, and re-layouts: 7.36 us -> 0.01 us
    pallas_call x1, Pallas kernels: 64.1 us -> 43 us  [exchange(): pl.pallas_call(exchange_kernel, out_shape=(pltpu.VMEM((USERS, HIST, 2 * D...]
    unnamed x18 -> x2, local copies, waits for them, and re-layouts: 7.36 us -> 0.01 us
    pallas_call x1, Pallas kernels: 4.59 us -> 3.79 us  [output(): pl.pallas_call(output_kernel, out_shape=(jax.ShapeDtypeStruct((USERS, HIS...]
where the time goes in v2:
time: 47.7 us; the launch traced here: 47.6 us
  Pallas kernels  46.7 us (98%)
  between operations  0.82 us (2%)
    pallas_call x1, Pallas kernels, exchange(): pl.pallas_call(exchange_kernel, out_shape=(pltpu.VMEM((USERS, HIST, 2 * D...  43 us
    pallas_call x1, Pallas kernels, output(): pl.pallas_call(output_kernel, out_shape=(jax.ShapeDtypeStruct((USERS, HIS...  3.79 us

profile of v2, /device:TPU:1, one launch (start us, length us, event | category | flops | bytes accessed | tf_op | source)
XLA Modules:
  0.0 47.6 jit_solution(7865133927151358633)
XLA Ops:
  0.6 0.0 copy-start
  0.6 43.0 %exchange.1 = (bf16[16,64,2048]{2,1,0:T(8,128)(2,1)S(1)}, bf16[512,1024]{1,0:T(8,128)(2,1)S(1)}, bf16[512,1024]{1,0:T(8,128)(2,1)S(1)}) custom-call(bf16[512,1024]{1,0:T(8,128)(2,1)} %bitcast.5, s32[1,16]{1,0:T(1,128)} %len_h.1, s32[1,16]{1,0:T(1,128)} %own_h.1, s32[1,1024]{1,0:T(1,128)} %ids_h.1, s32[1,8]{1,0:T(1,128)} %count_h.3, s32[1,8]{1,0:T(1,128)} %rown_h.1, ...), custom_call_target="tpu_custom_call" | custom-call | flops 13958643712 | bytes 20971520 | tf_op jit(solution)/shard_map/exchange/pallas_call | solution.py:254
  43.6 0.0 copy-done
  43.6 3.8 %output.1 = (bf16[16,64,2048]{2,1,0:T(8,128)(2,1)}, bf16[1024,1024]{1,0:T(8,128)(2,1)}) custom-call(bf16[16,64,2048]{2,1,0:T(8,128)(2,1)S(1)} %get-tuple-element.7.cache_in, bf16[512,1024]{1,0:T(8,128)(2,1)S(1)} %get-tuple-element.8.gated, bf16[512,1024]{1,0:T(8,128)(2,1)S(1)} %get-tuple-element.9.emb, bf16[1024,1024]{1,0:T(8,128)(2,1)S(1)} %copy-done, ...), custom_call_target="tpu_custom_call" | custom-call | flops 2147483648 | bytes 16777216 | tf_op jit(solution)/shard_map/output/pallas_call | solution.py:329
Async XLA Ops:
  0.6 43.0 %copy-start = (bf16[1024,1024]{1,0:T(8,128)(2,1)S(1)}, bf16[1024,1024]{1,0:T(8,128)(2,1)}, u32[]{:S(2)}) copy-start(bf16[1024,1024]{1,0:T(8,128)(2,1)} %wout.1) | copy-start | bytes 6291460

commit v3 on v2

v3 whole, which is shorter than its diff:
```python
import jax
import jax.numpy as jnp
from jax import lax
from jax.experimental import pallas as pl
from jax.experimental.pallas import tpu as pltpu
from jax.sharding import PartitionSpec as P

D = 1024
HEADS = 8
HEAD_DIM = 128
HIST = 64
CB = 128
USERS = 16
REQS = 8
ROWS = 512
LIVE = 512
CHUNK = (16, 16, 16, 16)
CHUNKS = len(CHUNK)
FIRST = tuple(sum(CHUNK[:q]) for q in range(CHUNKS))
LAST = CHUNKS - 1
WINDOW = 256
SCALE = HEAD_DIM ** (-0.5)
MESH = pl.DeviceIdType.MESH
F32 = jnp.float32
BF16 = jnp.bfloat16
I32 = jnp.int32

XY = [(2, 2), (0, 2), (2, 0), (3, 1), (1, 3), (3, 3), (1, 1), (2, 3), (3, 2), (2, 1), (1, 2), (3, 0), (0, 3), (1, 0), (0, 1)]
ZK = [(2, 0), (2, 1), (1, 0), (3, 0), (1, 1), (3, 1), (0, 1)]


def in_hbm(array):
    return pltpu.with_memory_space_constraint(array, pltpu.HBM)


def iota(shape, dim):
    return lax.broadcasted_iota(I32, shape, dim)


def silu(x):
    half = 0.5 * x
    return half + half * jnp.tanh(half)


def masked_silu(x, half_scale):
    half = x * half_scale
    return (half + half * jnp.tanh(half)).astype(BF16)


def norm(x):
    mean = jnp.sum(x, axis=-1, keepdims=True) * (1.0 / D)
    centred = x - mean
    spread = jnp.sum(centred * centred, axis=-1, keepdims=True) * (1.0 / D)
    return centred * lax.rsqrt(spread + 1e-06)


def dot(a, b):
    return jnp.dot(a, b, preferred_element_type=F32)


def dot_nt(a, b):
    return lax.dot_general(a, b, (((1,), (1,)), ((), ())), preferred_element_type=F32)


def cols(i, width):
    return pl.ds(pl.multiple_of(i * width, width), width)


def request_bounds(counts):
    lane = iota((1, REQS), 1)
    starts = [jnp.sum(jnp.where(lane < j, counts, 0.0), axis=1, keepdims=True) for j in range(REQS)]
    lengths = [jnp.sum(jnp.where(lane == j, counts, 0.0), axis=1, keepdims=True) for j in range(REQS)]
    return starts, lengths


def exchange_kernel(
    feats_h, len_h, own_h, ids_h, count_h, rown_h, rslot_h, table_h, wqu_h, wkv_h, wout_h,
    kv, emb, query, gate, att, asked, wkv, wout, mask, spread,
    feats, len_v, own_v, ids_v, count_v, rown_v, rslot_v, table, wqu,
    hn, pick0, pick1, pick2, pick3, send0, send1, send2, send3, recv0, recv1, recv2, recv3, slot_out, slot_in, select,
    stage0, stage1, stage2, stage3, back0, back1, back2, back3, kvr, onehot, cn, skv,
    load_sem, ss1, rs1, ss2, rs2, sss, rss,
):
    r = lax.axis_index("req")
    c = lax.axis_index("cache")
    z, k = r // 2, lax.rem(r, 2)
    y, x = c // 4, lax.rem(c, 4)
    pick = [pick0, pick1, pick2, pick3]
    send = [send0, send1, send2, send3]
    recv = [recv0, recv1, recv2, recv3]
    stage = [stage0, stage1, stage2, stage3]
    back = [back0, back1, back2, back3]

    def plane(offset):
        dy, dx = offset
        return lax.rem(y + dy, 4) * 4 + lax.rem(x + dx, 4)

    def column(offset):
        dz, dk = offset
        return lax.rem(z + dz, 4) * 2 + lax.rem(k + dk, 2)

    pairs = [
        (feats_h, feats), (len_h, len_v), (own_h, own_v), (count_h, count_v), (ids_h, ids_v), (rown_h, rown_v), (rslot_h, rslot_v),
        (table_h, table), (wqu_h, wqu), (wkv_h, wkv), (wout_h, wout),
    ]
    loads = [pltpu.make_async_copy(src, dst, load_sem.at[i]) for i, (src, dst) in enumerate(pairs)]
    for i in (1, 2, 0):
        loads[i].start()

    barrier = pltpu.get_barrier_semaphore()
    for offset in XY:
        pl.semaphore_signal(barrier, inc=1, device_id=(r, plane(offset)), device_id_type=MESH)
    for offset in ZK:
        pl.semaphore_signal(barrier, inc=1, device_id=(column(offset), c), device_id_type=MESH)

    loads[1].wait()
    loads[2].wait()
    lengths = len_v[...].astype(F32)
    owner = own_v[...]
    lane_j = iota((USERS, USERS), 1)
    mine = owner == iota((USERS, USERS), 0)
    order = jnp.sum(jnp.where(mine, lane_j.astype(F32), 0.0), axis=1, keepdims=True)
    length_of = jnp.sum(jnp.where(mine, lengths, 0.0), axis=1, keepdims=True)
    start_of = jnp.sum(jnp.where(lane_j.astype(F32) < order, lengths, 0.0), axis=1, keepdims=True)

    def build_pick(q):
        n = CHUNK[q]
        row = iota((n, ROWS), 1).astype(F32)
        step = iota((n, ROWS), 0).astype(F32) + float(FIRST[q])
        for o in range(USERS):
            place = row - start_of[o : o + 1, :]
            hit = jnp.logical_and(place == step, place < length_of[o : o + 1, :])
            pick[q][o * n : (o + 1) * n, :] = jnp.where(hit, 1.0, 0.0).astype(BF16)

    def slot_copy(i):
        to = column(ZK[i])
        return pltpu.make_async_remote_copy(
            src_ref=slot_out.at[to], dst_ref=slot_in.at[r], send_sem=sss.at[i], recv_sem=rss.at[i],
            device_id=(to, c), device_id_type=MESH,
        )

    def plane_copy(q, i):
        to = plane(XY[i])
        return pltpu.make_async_remote_copy(
            src_ref=send[q].at[cols(to, CHUNK[q]), :], dst_ref=recv[q].at[cols(c, CHUNK[q]), :],
            send_sem=ss1.at[q, i], recv_sem=rs1.at[q, i], device_id=(r, to), device_id_type=MESH,
        )

    def column_copy(q, i):
        to = column(ZK[i])
        return pltpu.make_async_remote_copy(
            src_ref=stage[q].at[cols(to, CHUNK[q]), :], dst_ref=back[q].at[cols(r, CHUNK[q]), :],
            send_sem=ss2.at[q, i], recv_sem=rs2.at[q, i], device_id=(to, c), device_id_type=MESH,
        )

    loads[0].wait()
    for i in range(ROWS // 64):
        rows = slice(i * 64, (i + 1) * 64)
        hn[rows, :] = norm(feats[rows, :].astype(F32)).astype(BF16)
    for q in range(CHUNKS):
        build_pick(q)
        send[q][...] = dot(pick[q][...], hn[...]).astype(BF16)
        if q == 0:
            pl.semaphore_wait(barrier, len(XY) + len(ZK))
        for i in range(len(XY)):
            plane_copy(q, i).start()
        if q == 0:
            for i in range(3, len(loads)):
                loads[i].start()
        own_rows = cols(c, CHUNK[q])
        recv[q][own_rows, :] = send[q][own_rows, :]

    for i in (3, 4, 5, 6):
        loads[i].wait()
    req_owner = rown_v[...]
    req_slot = rslot_v[...]
    for o in range(REQS):
        wanted = jnp.sum(jnp.where(req_owner == o, req_slot.astype(F32), 0.0), axis=1, keepdims=True)
        slot_out[o] = jnp.broadcast_to(wanted, (8, 128)).astype(I32)
    for i in range(len(ZK)):
        slot_copy(i).start()
    slot_in[r] = slot_out[r]

    starts, counts = request_bounds(count_v[...].astype(F32))
    packed = iota((LIVE, CB), 0).astype(F32)
    lane = iota((LIVE, CB), 1).astype(F32)
    id_sum = jnp.zeros((LIVE, CB), F32)
    owner_sum = jnp.zeros((LIVE, CB), F32)
    req_owner_f = req_owner.astype(F32)
    for j in range(REQS):
        place = packed - starts[j]
        hit = jnp.logical_and(place == lane, lane < counts[j])
        id_sum = id_sum + jnp.where(hit, ids_v[0:1, j * CB : (j + 1) * CB].astype(F32), 0.0)
        inside = jnp.logical_and(place >= 0.0, place < counts[j])
        owner_sum = owner_sum + jnp.where(inside, req_owner_f[:, j : j + 1], 0.0)
    mask[...] = jnp.where(owner_sum == (iota((LIVE, CB), 1) // CHUNK[1]).astype(F32), 0.5 * SCALE, 0.0)
    ids = jnp.sum(id_sum, axis=1, keepdims=True)
    for n in range(D // 128):
        word = (iota((LIVE, 128), 1) + n * 128).astype(F32)
        onehot[:, n * 128 : (n + 1) * 128] = jnp.where(ids == word, 1.0, 0.0).astype(BF16)

    loads[7].wait()
    emb[...] = dot(onehot[...], table[...]).astype(BF16)
    for i in range(LIVE // 64):
        rows = slice(i * 64, (i + 1) * 64)
        cn[rows, :] = norm(emb[rows, :].astype(F32)).astype(BF16)
    loads[8].wait()
    query[...] = silu(dot(cn[...], wqu[:, :D])).astype(BF16)
    gate[...] = silu(dot(cn[...], wqu[:, D:])).astype(BF16)
    loads[9].wait()
    skv[...] = silu(dot(cn[...], wkv[...])).astype(BF16)
    for h in range(HEADS):
        head = slice(h * HEAD_DIM, (h + 1) * HEAD_DIM)
        value = slice(D + h * HEAD_DIM, D + (h + 1) * HEAD_DIM)
        product = query[:, head].astype(F32) * skv[:, head].astype(F32)
        weight = silu(jnp.sum(product, axis=1, keepdims=True) * SCALE)
        att[:, head] = weight * skv[:, value].astype(F32)

    slot = iota((CB, WINDOW), 0).astype(F32)
    shifted = iota((CB, WINDOW), 1).astype(F32) - slot
    for j in range(REQS):
        base = jnp.minimum(jnp.floor(starts[j] * (1.0 / 16.0)) * 16.0, float(LIVE - WINDOW))
        hit = jnp.logical_and(shifted == starts[j] - base, slot < counts[j])
        spread[j * CB : (j + 1) * CB, :] = jnp.where(hit, 1.0, 0.0).astype(BF16)

    for i in range(len(ZK)):
        slot_copy(i).wait_recv()
    n = CHUNK[0]
    lane_row = iota((n, USERS * n), 1).astype(F32)
    step = iota((n, USERS * n), 0).astype(F32)
    for o in range(REQS):
        slot = slot_in[o][0:1, 0:1].astype(F32)
        hit = lane_row == slot * float(n) + step
        select[o * n : (o + 1) * n, :] = jnp.where(hit, 1.0, 0.0).astype(BF16)

    def attend_chunk(q):
        for i in range(len(ZK)):
            column_copy(q, i).wait_recv()
        keys = slice(0, REQS * CHUNK[q])
        kvr[keys, :] = silu(dot(back[q][...], wkv[...])).astype(BF16)
        for h in range(HEADS):
            head = slice(h * HEAD_DIM, (h + 1) * HEAD_DIM)
            value = slice(D + h * HEAD_DIM, D + (h + 1) * HEAD_DIM)
            weight = masked_silu(dot_nt(query[:, head], kvr[keys, head]), mask[...])
            att[:, head] += dot(weight, kvr[keys, value])

    for q in range(CHUNKS):
        n = CHUNK[q]
        for i in range(len(XY)):
            plane_copy(q, i).wait_recv()
        stage[q][...] = dot(select[...], recv[q][...]).astype(BF16)
        for i in range(len(ZK)):
            column_copy(q, i).start()
        own_rows = cols(r, n)
        back[q][own_rows, :] = stage[q][own_rows, :]
        block = silu(dot(recv[q][...], wkv[...])).astype(BF16)
        kv[:, FIRST[q] : FIRST[q] + n, :] = block.reshape(USERS, n, 2 * D)
        if q > 0:
            attend_chunk(q - 1)

    for i in range(len(ZK)):
        slot_copy(i).wait_send()
    for q in range(CHUNKS):
        for i in range(len(XY)):
            plane_copy(q, i).wait_send()
        for i in range(len(ZK)):
            column_copy(q, i).wait_send()
    loads[10].wait()
    for i in range(len(ZK)):
        column_copy(LAST, i).wait_recv()
    asked[...] = back[LAST][...]


def exchange(feats, lens, owners, ids, counts, req_owner, req_slot, table, w_qu, w_kv, w_out):
    any_spec = pl.BlockSpec(memory_space=pl.ANY)
    vmem = pltpu.VMEM
    sems = pltpu.SemaphoreType.DMA
    outs = (
        vmem((USERS, HIST, 2 * D), BF16), vmem((LIVE, D), BF16), vmem((LIVE, D), BF16), vmem((LIVE, D), BF16),
        vmem((LIVE, D), F32), vmem((REQS * CHUNK[LAST], D), BF16), vmem((D, 2 * D), BF16), vmem((D, D), BF16),
        vmem((LIVE, REQS * CHUNK[LAST]), F32), vmem((REQS * CB, WINDOW), BF16),
    )
    return pl.pallas_call(
        exchange_kernel,
        out_shape=outs,
        in_specs=[any_spec] * 11,
        out_specs=(pl.BlockSpec(memory_space=vmem),) * len(outs),
        scratch_shapes=[
            vmem((ROWS, D), BF16),
            vmem((1, USERS), I32), vmem((1, USERS), I32), vmem((1, REQS * CB), I32), vmem((1, REQS), I32),
            vmem((1, REQS), I32), vmem((1, REQS), I32),
            vmem((D, D), BF16), vmem((D, 2 * D), BF16),
            vmem((ROWS, D), BF16),
        ]
        + [vmem((USERS * n, ROWS), BF16) for n in CHUNK]
        + [vmem((USERS * n, D), BF16) for n in CHUNK]
        + [vmem((USERS * n, D), BF16) for n in CHUNK]
        + [vmem((REQS, 8, 128), I32), vmem((REQS, 8, 128), I32)]
        + [vmem((REQS * n, USERS * n), BF16) for n in CHUNK[:1]]
        + [vmem((REQS * n, D), BF16) for n in CHUNK]
        + [vmem((REQS * n, D), BF16) for n in CHUNK]
        + [
            vmem((REQS * max(CHUNK), 2 * D), BF16),
            vmem((LIVE, D), BF16), vmem((LIVE, D), BF16), vmem((LIVE, 2 * D), BF16),
            sems((11,)),
            sems((CHUNKS, len(XY))), sems((CHUNKS, len(XY))),
            sems((CHUNKS, len(ZK))), sems((CHUNKS, len(ZK))),
            sems((len(ZK),)), sems((len(ZK),)),
        ],
        compiler_params=pltpu.CompilerParams(collective_id=0, has_side_effects=True, vmem_limit_bytes=40 << 20),
        cost_estimate=pl.CostEstimate(flops=13 << 30, bytes_accessed=20 << 20, transcendentals=8 << 20),
        name="exchange",
    )(feats, lens, owners, ids, counts, req_owner, req_slot, table, w_qu, w_kv, w_out)


def output_kernel(
    cache_in, emb, query, gate, att, asked, wkv, wout, mask, spread, count_h,
    cache_out, cand_h,
    count_s, mixed, gated, res, out,
    sem, cache_sem, out_sem,
):
    load = pltpu.make_async_copy(count_h, count_s, sem)
    load.start()
    moves = [
        pltpu.make_async_copy(cache_in.at[pl.ds(i * 4, 4)], cache_out.at[pl.ds(i * 4, 4)], cache_sem.at[i]) for i in range(4)
    ]
    for copy in moves:
        copy.start()

    block = silu(dot(asked[...], wkv[...])).astype(BF16)
    for h in range(HEADS):
        head = slice(h * HEAD_DIM, (h + 1) * HEAD_DIM)
        value = slice(D + h * HEAD_DIM, D + (h + 1) * HEAD_DIM)
        weight = masked_silu(dot_nt(query[:, head], block[:, head]), mask[...])
        mixed[:, head] = att[:, head] + dot(weight, block[:, value])
    for i in range(LIVE // 64):
        rows = slice(i * 64, (i + 1) * 64)
        gated[rows, :] = (norm(mixed[rows, :]) * gate[rows, :].astype(F32)).astype(BF16)
    res[...] = (dot(gated[...], wout[...]) + emb[...].astype(F32)).astype(BF16)

    def out_copy(j):
        rows = pl.ds(j * CB, CB)
        return pltpu.make_async_copy(out.at[rows], cand_h.at[rows], out_sem.at[j])

    load.wait()
    start = jnp.int32(0)
    for j in range(REQS):
        base = jnp.minimum((start // 16) * 16, LIVE - WINDOW)
        window = pl.ds(pl.multiple_of(base, 16), WINDOW)
        out[j * CB : (j + 1) * CB, :] = dot(spread[j * CB : (j + 1) * CB, :], res[window, :]).astype(BF16)
        out_copy(j).start()
        start = start + count_s[0, j]
    for j in range(REQS):
        out_copy(j).wait()
    for copy in moves:
        copy.wait()


def output(cache, emb, query, gate, att, asked, w_kv, w_out, mask, spread, counts):
    any_spec = pl.BlockSpec(memory_space=pl.ANY)
    vmem = pltpu.VMEM
    return pl.pallas_call(
        output_kernel,
        out_shape=(
            jax.ShapeDtypeStruct((USERS, HIST, 2 * D), BF16),
            jax.ShapeDtypeStruct((REQS * CB, D), BF16),
        ),
        in_specs=[pl.BlockSpec(memory_space=vmem)] * 10 + [any_spec],
        out_specs=(any_spec,) * 2,
        scratch_shapes=[
            pltpu.SMEM((1, REQS), I32),
            vmem((LIVE, D), F32), vmem((LIVE, D), BF16), vmem((LIVE, D), BF16), vmem((REQS * CB, D), BF16),
            pltpu.SemaphoreType.DMA, pltpu.SemaphoreType.DMA((4,)), pltpu.SemaphoreType.DMA((REQS,)),
        ],
        compiler_params=pltpu.CompilerParams(vmem_limit_bytes=24 << 20),
        cost_estimate=pl.CostEstimate(flops=3 << 30, bytes_accessed=16 << 20, transcendentals=0),
        name="output",
    )(cache, emb, query, gate, att, asked, w_kv, w_out, mask, spread, in_hbm(counts))


def body(event_feats, hist_len, user_owner, cand_ids, cand_count, req_owner, req_slot, table, w_qu, w_kv, w_out):
    held = exchange(
        *(in_hbm(a) for a in (event_feats[0], hist_len, user_owner, cand_ids, cand_count, req_owner, req_slot, table, w_qu, w_kv, w_out))
    )
    cache, cand_out = output(*held, cand_count)
    return (cache[None], cand_out[None])


def solution(mesh):
    in_specs = (
        P(("req", "cache"), None, None),
        P(("req", "cache"), None),
        P(("req", "cache"), None),
        P(("req", "cache"), None),
        P(("req", "cache"), None),
        P(("req", "cache"), None),
        P(("req", "cache"), None),
        P(),
        P(),
        P(),
        P(),
    )
    out_specs = (P(("req", "cache"), None, None, None), P(("req", "cache"), None, None))
    return jax.shard_map(body, mesh=mesh, in_specs=in_specs, out_specs=out_specs, check_vma=False)
```

time: 47.7 us -> 46.2 us (0.969)
  Pallas kernels: 46.7 us -> 45.2 us
    pallas_call x1, Pallas kernels: 43 us -> 40.3 us  [exchange(): pl.pallas_call(exchange_kernel, out_shape=outs, in_specs=[any_spec] * 11,...]
    pallas_call x1, Pallas kernels: 3.79 us -> 4.88 us  [output(): pl.pallas_call(output_kernel, out_shape=(jax.ShapeDtypeStruct((USERS, HIS...]
where the time goes in v3:
time: 46.2 us; the launch traced here: 46 us
  Pallas kernels  45.2 us (98%)
  between operations  0.8 us (2%)
    pallas_call x1, Pallas kernels, exchange(): pl.pallas_call(exchange_kernel, out_shape=outs, in_specs=[any_spec] * 11,...  40.3 us
    pallas_call x1, Pallas kernels, output(): pl.pallas_call(output_kernel, out_shape=(jax.ShapeDtypeStruct((USERS, HIS...  4.88 us

profile of v3, /device:TPU:1, one launch (start us, length us, event | category | flops | bytes accessed | tf_op | source)
XLA Modules:
  0.0 46.0 jit_solution(3742872565857173186)
XLA Ops:
  0.6 40.3 %exchange.1 = (bf16[16,64,2048]{2,1,0:T(8,128)(2,1)S(1)}, bf16[512,1024]{1,0:T(8,128)(2,1)S(1)}, bf16[512,1024]{1,0:T(8,128)(2,1)S(1)}, bf16[512,1024]{1,0:T(8,1...) custom-call(bf16[512,1024]{1,0:T(8,128)(2,1)} %bitcast.5, ...), custom_call_target="tpu_custom_call" | custom-call | flops 13958643712 | bytes 20971520 | tf_op jit(solution)/shard_map/exchange/pallas_call | solution.py:283
  41.0 4.9 %output.1 = (bf16[16,64,2048]{2,1,0:T(8,128)(2,1)}, bf16[1024,1024]{1,0:T(8,128)(2,1)}) custom-call(bf16[16,64,2048]{2,1,0:T(8,128)(2,1)S(1)} %get-tuple-element.14.cache_in, bf16[512,1024]{1,0:T(8,128)(2,1)S(1)} %get-tuple-element.15.emb, bf16[512,1024]{1,0:T(8,128)(2,1)S(1)} %get-tuple-element.16.query, bf16[512,1024]{1,0:T(8,128)(2,1)S(1)} %get-tuple-element.17.gate, ...), custom_call_target="tpu_custom_call" | custom-call | flops 3221225472 | bytes 16777216 | tf_op jit(solution)/shard_map/output/pallas_call | solution.py:362

commit v4 on v3

--- a/solution.py
+++ b/solution.py
@@ -25,7 +25,7 @@
 BF16 = jnp.bfloat16
 I32 = jnp.int32
 
-XY = [(2, 2), (0, 2), (2, 0), (3, 1), (1, 3), (3, 3), (1, 1), (2, 3), (3, 2), (2, 1), (1, 2), (3, 0), (0, 3), (1, 0), (0, 1)]
+XY = [(2, 2), (0, 2), (2, 0), (1, 1), (3, 1), (3, 3), (1, 3), (1, 2), (2, 1), (3, 2), (2, 3), (3, 0), (1, 0), (0, 1), (0, 3)]
 ZK = [(2, 0), (2, 1), (1, 0), (3, 0), (1, 1), (3, 1), (0, 1)]
 
 
@@ -328,14 +328,22 @@
         copy.start()
 
     block = silu(dot(asked[...], wkv[...])).astype(BF16)
+    total = jnp.zeros((LIVE, HEAD_DIM), F32)
+    squares = jnp.zeros((LIVE, HEAD_DIM), F32)
     for h in range(HEADS):
         head = slice(h * HEAD_DIM, (h + 1) * HEAD_DIM)
         value = slice(D + h * HEAD_DIM, D + (h + 1) * HEAD_DIM)
         weight = masked_silu(dot_nt(query[:, head], block[:, head]), mask[...])
-        mixed[:, head] = att[:, head] + dot(weight, block[:, value])
+        part = att[:, head] + dot(weight, block[:, value])
+        mixed[:, head] = part
+        total = total + part
+        squares = squares + part * part
+    mean = jnp.sum(total, axis=1, keepdims=True) * (1.0 / D)
+    spread_of = jnp.sum(squares, axis=1, keepdims=True) * (1.0 / D) - mean * mean
+    scale = lax.rsqrt(jnp.maximum(spread_of, 0.0) + 1e-06)
     for i in range(LIVE // 64):
         rows = slice(i * 64, (i + 1) * 64)
-        gated[rows, :] = (norm(mixed[rows, :]) * gate[rows, :].astype(F32)).astype(BF16)
+        gated[rows, :] = ((mixed[rows, :] - mean[rows, :]) * (scale[rows, :] * gate[rows, :].astype(F32))).astype(BF16)
     res[...] = (dot(gated[...], wout[...]) + emb[...].astype(F32)).astype(BF16)
 
     def out_copy(j):

time: 46.2 us -> 45.4 us (0.983)
  Pallas kernels: 45.2 us -> 44.5 us
where the time goes in v4:
time: 45.4 us; the launch traced here: 45.3 us
  Pallas kernels  44.5 us (98%)
  between operations  0.8 us (2%)
    pallas_call x1, Pallas kernels, exchange(): pl.pallas_call(exchange_kernel, out_shape=outs, in_specs=[any_spec] * 11,...  39.9 us
    pallas_call x1, Pallas kernels, output(): pl.pallas_call(output_kernel, out_shape=(jax.ShapeDtypeStruct((USERS, HIS...  4.59 us

profile of v4, /device:TPU:1, one launch (start us, length us, event | category | flops | bytes accessed | tf_op | source)
XLA Modules:
  0.0 45.3 jit_solution(17922842281133354527)
XLA Ops:
  0.6 39.9 %exchange.1 = (bf16[16,64,2048]{2,1,0:T(8,128)(2,1)S(1)}, bf16[512,1024]{1,0:T(8,128)(2,1)S(1)}, bf16[512,1024]{1,0:T(8,128)(2,1)S(1)}, bf16[512,1024]{1,0:T(8,1...) custom-call(bf16[512,1024]{1,0:T(8,128)(2,1)} %bitcast.5, ...), custom_call_target="tpu_custom_call" | custom-call | flops 13958643712 | bytes 20971520 | tf_op jit(solution)/shard_map/exchange/pallas_call | solution.py:283
  40.5 4.6 %output.1 = (bf16[16,64,2048]{2,1,0:T(8,128)(2,1)}, bf16[1024,1024]{1,0:T(8,128)(2,1)}) custom-call(bf16[16,64,2048]{2,1,0:T(8,128)(2,1)S(1)} %get-tuple-element.14.cache_in, bf16[512,1024]{1,0:T(8,128)(2,1)S(1)} %get-tuple-element.15.emb, bf16[512,1024]{1,0:T(8,128)(2,1)S(1)} %get-tuple-element.16.query, bf16[512,1024]{1,0:T(8,128)(2,1)S(1)} %get-tuple-element.17.gate, ...), custom_call_target="tpu_custom_call" | custom-call | flops 3221225472 | bytes 16777216 | tf_op jit(solution)/shard_map/output/pallas_call | solution.py:370

commit v5 on v4

--- a/solution.py
+++ b/solution.py
@@ -341,10 +341,13 @@
     mean = jnp.sum(total, axis=1, keepdims=True) * (1.0 / D)
     spread_of = jnp.sum(squares, axis=1, keepdims=True) * (1.0 / D) - mean * mean
     scale = lax.rsqrt(jnp.maximum(spread_of, 0.0) + 1e-06)
-    for i in range(LIVE // 64):
-        rows = slice(i * 64, (i + 1) * 64)
-        gated[rows, :] = ((mixed[rows, :] - mean[rows, :]) * (scale[rows, :] * gate[rows, :].astype(F32))).astype(BF16)
-    res[...] = (dot(gated[...], wout[...]) + emb[...].astype(F32)).astype(BF16)
+    for half in range(2):
+        part_rows = slice(half * LIVE // 2, (half + 1) * LIVE // 2)
+        for i in range(LIVE // 128):
+            first = half * LIVE // 2 + i * 64
+            rows = slice(first, first + 64)
+            gated[rows, :] = ((mixed[rows, :] - mean[rows, :]) * (scale[rows, :] * gate[rows, :].astype(F32))).astype(BF16)
+        res[part_rows, :] = (dot(gated[part_rows, :], wout[...]) + emb[part_rows, :].astype(F32)).astype(BF16)
 
     def out_copy(j):
         rows = pl.ds(j * CB, CB)

time: 45.4 us -> 45.5 us (level)
  no operation moved by 1% of the time
where the time goes in v5:
time: 45.5 us; the launch traced here: 45.3 us
  Pallas kernels  44.5 us (98%)
  between operations  0.8 us (2%)
    pallas_call x1, Pallas kernels, exchange(): pl.pallas_call(exchange_kernel, out_shape=outs, in_specs=[any_spec] * 11,...  39.9 us
    pallas_call x1, Pallas kernels, output(): pl.pallas_call(output_kernel, out_shape=(jax.ShapeDtypeStruct((USERS, HIS...  4.61 us

profile of v5, /device:TPU:1, one launch (start us, length us, event | category | flops | bytes accessed | tf_op | source)
XLA Modules:
  0.0 45.3 jit_solution(15475649173662305193)
XLA Ops:
  0.6 39.9 %exchange.1 = (bf16[16,64,2048]{2,1,0:T(8,128)(2,1)S(1)}, bf16[512,1024]{1,0:T(8,128)(2,1)S(1)}, bf16[512,1024]{1,0:T(8,128)(2,1)S(1)}, bf16[512,1024]{1,0:T(8,1...) custom-call(bf16[512,1024]{1,0:T(8,128)(2,1)} %bitcast.5, ...), custom_call_target="tpu_custom_call" | custom-call | flops 13958643712 | bytes 20971520 | tf_op jit(solution)/shard_map/exchange/pallas_call | solution.py:283
  40.5 4.6 %output.1 = (bf16[16,64,2048]{2,1,0:T(8,128)(2,1)}, bf16[1024,1024]{1,0:T(8,128)(2,1)}) custom-call(bf16[16,64,2048]{2,1,0:T(8,128)(2,1)S(1)} %get-tuple-element.14.cache_in, bf16[512,1024]{1,0:T(8,128)(2,1)S(1)} %get-tuple-element.15.emb, bf16[512,1024]{1,0:T(8,128)(2,1)S(1)} %get-tuple-element.16.query, bf16[512,1024]{1,0:T(8,128)(2,1)S(1)} %get-tuple-element.17.gate, ...), custom_call_target="tpu_custom_call" | custom-call | flops 3221225472 | bytes 16777216 | tf_op jit(solution)/shard_map/output/pallas_call | solution.py:373
